TPU v7x, 256 devices: a whole 4x4x8 slice. The times are simulated.
256 devices in a mesh: gx: 32 (over z_lo, y, core), gy: 8 (over z_hi, x).
Axes of the slice: x: 4, y: 4, z: 8 (z_hi: 2, z_lo: 4; z = z_hi * 4 + z_lo), core: 2. Of those that a mesh axis runs over, the one named last changes fastest.
Arguments:
- child_state: float32 [5, 32, 512, 1024], P(None, None, 'gx', 'gy'), may hold values from -6 to 6
- cotangent: float32 [5, 32, 512, 1024], P(None, None, 'gx', 'gy'), may hold values from -6 to 6
- diffusivity: float32 [32, 512, 1024], P(None, 'gx', 'gy'), may hold values from 0.01 to 0.16
- field_mix: float32 [5, 5], replicated, may hold values from -2.5 to 2.5
- parent_we: float32 [2, 5, 128, 1024], P(None, None, 'gx', 'gy'), may hold values from -6 to 6
- parent_sn: float32 [2, 5, 128, 512], P(None, None, 'gy', 'gx'), may hold values from -6 to 6
- terrain_we: int32 [2, 1024], P(None, 'gy'), may hold values from 0 to 96, as said below
- terrain_sn: int32 [2, 512], P(None, 'gx'), may hold values from 0 to 96, as said below
- relax_width: int32 [1], replicated, may hold values from 4 to 15
Outputs:
- child_final: float32 [5, 32, 512, 1024], P(None, None, 'gx', 'gy')
- grad_state: float32 [5, 32, 512, 1024], P(None, None, 'gx', 'gy')
- grad_we: float32 [2, 5, 128, 1024], P(None, None, 'gx', 'gy')
- grad_sn: float32 [2, 5, 128, 512], P(None, None, 'gy', 'gx')
Inputs may be any that keep to these rules, and one draw needn't show every extreme that they name: `terrain_we`: on each edge some column has the largest value 128 - 32. `terrain_sn`: on each edge some column has the largest value 128 - 32.
All inputs are finite; a program needn't handle non-finite values.
Results may differ from a plain program's by a relative error of at most 0.000084.
Values sent between devices are 32-bit elements; how exact they have to be, the bound alone decides.
A program may use at most 128 MiB of HBM per device.

v0:
```python
import jax
import jax.numpy as jnp
from jax import lax
from jax.sharding import PartitionSpec as P

near_weight = 4.0 / 3.0
far_weight = -1.0 / 12.0
coupling = 0.25
highest = lax.Precision.HIGHEST


def with_halo(cells, sides, width):
    for axis, dim in sides:
        count = lax.axis_size(axis)
        ends = count - 1
        head = lax.slice_in_dim(cells, 0, width, axis=dim)
        tail = lax.slice_in_dim(cells, cells.shape[dim] - width, cells.shape[dim], axis=dim)
        cells = jnp.concatenate(
            [
                lax.ppermute(tail, axis, [(i, (i + 1) % count) for i in range(ends)]),
                cells,
                lax.ppermute(head, axis, [((i + 1) % count, i) for i in range(ends)]),
            ],
            axis=dim,
        )
    return cells


def laplace(padded):
    centre_cell = padded[..., 2:-2, 2:-2]
    summed = near_weight * (
        padded[..., 3:-1, 2:-2]
        + padded[..., 1:-3, 2:-2]
        + padded[..., 2:-2, 3:-1]
        + padded[..., 2:-2, 1:-3]
    )
    summed = summed + far_weight * (
        padded[..., 4:, 2:-2]
        + padded[..., :-4, 2:-2]
        + padded[..., 2:-2, 4:]
        + padded[..., 2:-2, :-4]
    )
    return summed - 5.0 * centre_cell


def zone_ramp(position, length, zone_width):
    distance = jnp.minimum(position, length - 1 - position)
    return jnp.maximum(zone_width - distance, 0).astype(jnp.float32) / (zone_width + 1).astype(
        jnp.float32
    )


def level_weights(terrain, level_count, child_count):
    child_level = jnp.arange(child_count, dtype=jnp.int32)
    base_level = terrain[:, None, :] + child_level[None, :, None]
    parent = jnp.arange(level_count, dtype=jnp.int32)
    return (parent[None, None, :, None] == base_level[:, :, None, :]).astype(jnp.float32)


def fold_with(weights, section):
    return jnp.einsum("eflc,eklc->efkc", section, weights, precision=highest)


def mix_ahead(field_mix, values):
    return jnp.einsum("fg,gkxy->fkxy", field_mix, values, precision=highest)


def mix_back(field_mix, values):
    return jnp.einsum("gf,gkxy->fkxy", field_mix, values, precision=highest)


def body(
    child_state,
    cotangent,
    diffusivity,
    field_mix,
    parent_we,
    parent_sn,
    terrain_we,
    terrain_sn,
    relax_width,
):
    fields, levels, cols_x, rows_y = child_state.shape
    total_x = cols_x * lax.axis_size("gx")
    total_y = rows_y * lax.axis_size("gy")
    start_x = lax.axis_index("gx") * cols_x
    start_y = lax.axis_index("gy") * rows_y
    position_x = start_x + jnp.arange(cols_x, dtype=jnp.int32)
    position_y = start_y + jnp.arange(rows_y, dtype=jnp.int32)
    zone_width = relax_width[0]
    ramp_x = zone_ramp(position_x, total_x, zone_width)[None, None, :, None]
    ramp_y = zone_ramp(position_y, total_y, zone_width)[None, None, None, :]
    west_side = (position_x < total_x // 2)[None, None, :, None]
    south_side = (position_y < total_y // 2)[None, None, None, :]
    levels_we = parent_we.shape[2]
    levels_sn = parent_sn.shape[2]
    weights_we = level_weights(terrain_we, levels_we * lax.axis_size("gx"), levels)
    weights_sn = level_weights(terrain_sn, levels_sn * lax.axis_size("gy"), levels)
    bound_we = fold_with(weights_we, lax.all_gather(parent_we, "gx", axis=2, tiled=True))
    bound_sn = fold_with(weights_sn, lax.all_gather(parent_sn, "gy", axis=2, tiled=True))
    edge_x = jnp.where(west_side, bound_we[0][:, :, None, :], bound_we[1][:, :, None, :])
    edge_y = jnp.where(south_side, bound_sn[0][:, :, :, None], bound_sn[1][:, :, :, None])

    def finish_step(values, padded):
        stepped = (
            values + diffusivity[None] * laplace(padded) + coupling * mix_ahead(field_mix, values)
        )
        across = (1.0 - ramp_x) * stepped + ramp_x * edge_x
        return (1.0 - ramp_y) * across + ramp_y * edge_y

    def weigh_back(incoming):
        return (1.0 - ramp_y) * (1.0 - ramp_x) * incoming

    def finish_back(pulled, padded):
        return pulled + laplace(padded) + coupling * mix_back(field_mix, pulled)

    def advance(values):
        padded = with_halo(values, (("gx", 2), ("gy", 3)), 2)
        return finish_step(values, padded)

    child_final = advance(advance(child_state))

    def retreat(incoming):
        pulled = weigh_back(incoming)
        padded = with_halo(diffusivity[None] * pulled, (("gx", 2), ("gy", 3)), 2)
        return finish_back(pulled, padded)

    middle = retreat(cotangent)
    grad_state = retreat(middle)
    carried = cotangent + middle
    push_x = (1.0 - ramp_y) * ramp_x * carried
    push_y = ramp_y * carried
    d_we = jnp.stack(
        [
            jnp.sum(jnp.where(west_side, push_x, 0.0), axis=2),
            jnp.sum(jnp.where(west_side, 0.0, push_x), axis=2),
        ]
    )
    d_sn = jnp.stack(
        [
            jnp.sum(jnp.where(south_side, push_y, 0.0), axis=3),
            jnp.sum(jnp.where(south_side, 0.0, push_y), axis=3),
        ]
    )
    whole_we = jnp.einsum("efkc,eklc->eflc", d_we, weights_we, precision=highest)
    whole_sn = jnp.einsum("efkc,eklc->eflc", d_sn, weights_sn, precision=highest)
    grad_we = lax.psum_scatter(whole_we, "gx", scatter_dimension=2, tiled=True)
    grad_sn = lax.psum_scatter(whole_sn, "gy", scatter_dimension=2, tiled=True)
    return (child_final, grad_state, grad_we, grad_sn)


def solution(mesh):
    return jax.shard_map(
        body,
        mesh=mesh,
        in_specs=(
            P(None, None, "gx", "gy"),
            P(None, None, "gx", "gy"),
            P(None, "gx", "gy"),
            P(),
            P(None, None, "gx", "gy"),
            P(None, None, "gy", "gx"),
            P(None, "gy"),
            P(None, "gx"),
            P(),
        ),
        out_specs=(
            P(None, None, "gx", "gy"),
            P(None, None, "gx", "gy"),
            P(None, None, "gx", "gy"),
            P(None, None, "gy", "gx"),
        ),
        check_vma=False,
    )
```

profile of v0, /device:TPU:6, one launch (start us, length us, event | category | flops | bytes accessed | tf_op | source)
XLA Modules:
  0.0 648.5 jit_solution(7068104871917820712)
XLA Ops:
  20.6 4.3 collective-permute-start.9
  25.0 45.7 %all_gather.7 = f32[2,5,128,16]{3,0,1,2:T(2,128)S(1)} all-gather(f32[2,5,16,16]{3,0,1,2:T(2,128)S(1)} %copy.98), channel_id=1, replica_groups=mesh['gx'=32,'gy'=8] {'gy'}, dimensions={2}, use_global_device_ids=true | all-gather | bytes 92160 | tf_op jit(solution)/shard_map/all_gather | solution.py:100
  71.8 46.6 %all_gather.6 = f32[2,5,128,128]{3,0,1,2:T(2,128)S(1)} all-gather(f32[2,5,4,128]{3,0,1,2:T(2,128)S(1)} %copy.94), channel_id=1, replica_groups=mesh['gx'=32,'gy'=8] {'gx'}, dimensions={2}, use_global_device_ids=true | all-gather | bytes 675840 | tf_op jit(solution)/shard_map/all_gather | solution.py:99
  118.4 9.6 %copy.95 = f32[2,5,128,128]{1,2,3,0:T(8,128)} copy(f32[2,5,128,128]{3,0,1,2:T(2,128)S(1)} %all_gather.6) | data formatting | bytes 1310720 | tf_op jit(solution)/shard_map/all_gather | solution.py:99
  128.2 17.2 %fusion.70 = f32[2,5,32,128]{2,1,3,0:T(8,128)S(1)} fusion(f32[2,5,128,128]{1,2,3,0:T(8,128)} %copy.95, s32[2,32,128]{1,2,0:T(8,128)S(1)} %iota_add_fusion), kind=kOutput, calls=%fused_computation.123 | convolution fusion | flops 63963136 | bytes 851968 | tf_op jit(solution)/shard_map/eflc,eklc->efkc/dot_general | solution.py:61
  165.0 6.5 %collective-permute-start.3 = (f32[5,32,20,2]{1,3,2,0:T(2,128)}, f32[5,32,20,2]{1,3,2,0:T(2,128)}, u32[]{:S(2)}, u32[]{:S(2)}) collective-permute-start(f32[5,32,20,2]{1,3,2,0:T(2,128)} %copy.89), channel_id=1, source_target_pairs={{0,1},{1,2},{2,3},{3,4},{4,5},{5,6},{6,7},{8,9},{9,10},{10,11},{11... | collective-permute-start | bytes 76808 | tf_op jit(solution)/shard_map/ppermute | solution.py:20
  185.5 9.9 %collective-permute-start.11 = (f32[5,32,20,2]{1,3,2,0:T(2,128)}, f32[5,32,20,2]{1,3,2,0:T(2,128)}, u32[]{:S(2)}, u32[]{:S(2)}) collective-permute-start(f32[5,32,20,2]{1,3,2,0:T(2,128)} %copy.109), channel_id=1, source_target_pairs={{0,1},{1,2},{2,3},{3,4},{4,5},{5,6},{6,7},{8,9},{9,10},{10,11},{11... | collective-permute-start | bytes 76808 | tf_op jit(solution)/shard_map/ppermute | solution.py:20
  200.7 4.3 copy.90
  205.0 4.3 copy.88
  209.3 12.3 %fusion.61 = f32[5,32,16,128]{3,0,2,1:T(8,128)S(1)} fusion(f32[5,32,20,128]{3,0,2,1:T(8,128)S(1)} %get-tuple-element.49, f32[5,32,20,2]{3,0,2,1:T(8,128)} %copy.90, f32[5,32,20,2]{3,0,2,1:T(8,128)} %copy.88, f32[5,32,18,128]{3,0,2,1:T(8,128)} %copy-done.24, f32[5,32,18,128]{3,0,2,1:T(8,128)} %copy-done.8, f32[5,32,16,128]{3,2,1,0:T(8,128)} %param.9, ...), kind=kOutput, calls=%fused_computation.104 | convolution fusion | flops 28508160 | bytes 19749988 | tf_op jit(solution)/shard_map/fg,gkxy->fkxy/dot_general | solution.py:65
  226.6 4.3 copy.110
  230.9 4.3 copy.108
  235.2 15.7 %select_reduce_fusion.1 = (f32[5,32,16]{0,2,1:T(8,128)}, f32[5,32,16]{0,2,1:T(8,128)}, f32[5,32,128]{2,0,1:T(8,128)}, f32[5,32,128]{2,0,1:T(8,128)}, f32[5,32,16...) fusion(f32[128]{0:T(128)} %get-tuple-element.23, pred[128]{0:T(512)(128)(4,1)} %fusion.96, ...), kind=kOutput, calls=%fused_computation.113 | convolution fusion | flops 34360320 | bytes 8194704 | tf_op jit(solution)/shard_map/gf,gkxy->fkxy/dot_general | solution.py:69
  261.7 3.7 fusion.71
  266.7 103.3 %all-reduce.7.cloned.1.call-done = f32[2,5,128,16]{3,0,1,2:T(2,128)} async-done(((f32[2,5,128,16]{3,0,1,2:T(2,128)}), f32[2,5,128,16]{3,0,1,2:T(2,128)}) %all-reduce.7.cloned.1.call-update) | async-done | bytes 81936
  378.5 4.1 collective-permute-start.7
  393.4 9.9 %collective-permute-start.15 = (f32[5,32,20,2]{1,3,2,0:T(2,128)S(1)}, f32[5,32,20,2]{1,3,2,0:T(2,128)}, u32[]{:S(2)}, u32[]{:S(2)}) collective-permute-start(f32[5,32,20,2]{1,3,2,0:T(2,128)S(1)} %copy.114), channel_id=1, source_target_pairs={{0,1},{1,2},{2,3},{3,4},{4,5},{5,6},{6,7},{8,9},{9,10},{10,11},{11... | collective-permute-start | bytes 76808 | tf_op jit(solution)/shard_map/ppermute | solution.py:20
  407.6 4.3 copy.105
  411.8 4.3 copy.103
  416.3 9.8 %fusion.36 = f32[5,32,16,128]{3,0,2,1:T(8,128)S(1)} fusion(f32[5,32,16,128]{3,0,2,1:T(8,128)S(1)} %copy-done.5, f32[5,32,2,128]{3,0,2,1:T(8,128)} %collective-permute-done.5, f32[5,32,2,128]{3,0,2,1:T(8,128)} %collective-permute-done.4, f32[5,32,20,2]{3,0,2,1:T(8,128)} %copy.105, f32[5,32,20,2]{3,0,2,1:T(8,128)} %copy.103, f32[5,32,16]{0,2,1:T(8,128)S(1)} %copy-done.16, ...), kind=kOutput, calls=%fused_computation.54 | convolution fusion | flops 32440320 | bytes 6939648 | tf_op jit(solution)/shard_map/fg,gkxy->fkxy/dot_general | solution.py:65
  427.4 4.4 copy.115
  431.8 4.3 copy.113
  436.1 10.5 %fusion.13 = f32[5,32,16,128]{3,0,2,1:T(8,128)S(1)} fusion(f32[5,32,2,128]{3,0,2,1:T(8,128)S(1)} %collective-permute-done.13, f32[5,32,16,128]{3,0,2,1:T(8,128)S(1)} %copy-done.7, f32[5,32,2,128]{3,0,2,1:T(8,128)} %collective-permute-done.12, f32[5,32,20,2]{3,0,2,1:T(8,128)} %copy.115, f32[5,32,20,2]{3,0,2,1:T(8,128)} %copy.113, ...), kind=kOutput, calls=%fused_computation.31 | convolution fusion | flops 30146560 | bytes 13389824 | tf_op jit(solution)/shard_map/gf,gkxy->fkxy/dot_general | solution.py:69
  447.9 192.2 %all-reduce.5.cloned.1.call-done = f32[2,5,128,128]{3,0,1,2:T(2,128)} async-done(((f32[2,5,128,128]{3,0,1,2:T(2,128)}), f32[2,5,128,128]{3,0,1,2:T(2,128)}) %all-reduce.5.cloned.1.call-update) | async-done | bytes 655376
  (166 shorter events, 95.8 us)
Async XLA Ops:
  7.2 202.2 %copy-start = (f32[5,5]{1,0:T(8,128)S(1)}, f32[5,5]{1,0:T(8,128)}, u32[]{:S(2)}) copy-start(f32[5,5]{1,0:T(8,128)} %param.12) | copy-start | bytes 304
  7.2 362.8 %all-reduce.7.cloned.1.call-start = ((), (), s32[]{:S(2)}) async-start(), calls=%async_computation.1 | async-start | bytes 1310720
  8.8 143.7 %collective-permute-start.1 = (f32[5,32,2,128]{3,0,2,1:T(8,128)S(1)}, f32[5,32,2,128]{3,0,2,1:T(8,128)}, u32[]{:S(2)}, u32[]{:S(2)}) collective-permute-start(f32[5,32,2,128]{3,0,2,1:T(8,128)S(1)} %copy.157), channel_id=1, source_target_pairs={{0,8},{8,16},{16,24},{24,32},{32,40},{40,48},{48,56},{56,64},{64,7... | collective-permute-start | bytes 491528 | tf_op jit(solution)/shard_map/ppermute | solution.py:20
  12.1 143.6 %collective-permute-start = (f32[5,32,2,128]{3,0,2,1:T(8,128)}, f32[5,32,2,128]{3,0,2,1:T(8,128)S(1)}, u32[]{:S(2)}, u32[]{:S(2)}) collective-permute-start(f32[5,32,2,128]{3,0,2,1:T(8,128)} %copy.158), channel_id=1, source_target_pairs={{8,0},{16,8},{24,16},{32,24},{40,32},{48,40},{56,48},{64,56},{72,6... | collective-permute-start | bytes 491528 | tf_op jit(solution)/shard_map/ppermute | solution.py:22
  18.5 52.6 %copy-start.33 = (s32[2,16]{1,0:T(2,128)S(1)}, s32[2,16]{1,0:T(2,128)}, u32[]{:S(2)}) copy-start(s32[2,16]{1,0:T(2,128)} %param.16) | copy-start | bytes 388
  18.5 53.3 %copy-start.25 = (f32[2,5,4,128]{3,2,1,0:T(4,128)S(1)}, f32[2,5,4,128]{3,2,1,0:T(4,128)}, u32[]{:S(2)}) copy-start(f32[2,5,4,128]{3,2,1,0:T(4,128)} %param.13) | copy-start | bytes 61444
  19.3 157.5 %collective-permute-start.8 = (f32[5,32,2,128]{3,0,2,1:T(8,128)}, f32[5,32,2,128]{3,0,2,1:T(8,128)S(1)}, u32[]{:S(2)}, u32[]{:S(2)}) collective-permute-start(f32[5,32,2,128]{3,0,2,1:T(8,128)} %get-tuple-element.37), channel_id=1, source_target_pairs={{8,0},{16,8},{24,16},{32,24},{40,32},{48,40},{56,48},{64,56},{72,6... | collective-permute-start | bytes 491528 | tf_op jit(solution)/shard_map/ppermute | solution.py:22
  20.6 156.3 %collective-permute-start.9 = (f32[5,32,2,128]{3,0,2,1:T(8,128)}, f32[5,32,2,128]{3,0,2,1:T(8,128)S(1)}, u32[]{:S(2)}, u32[]{:S(2)}) collective-permute-start(f32[5,32,2,128]{3,0,2,1:T(8,128)} %get-tuple-element.38), channel_id=1, source_target_pairs={{0,8},{8,16},{16,24},{24,32},{32,40},{40,48},{48,56},{56,64},{64,7... | collective-permute-start | bytes 491528 | tf_op jit(solution)/shard_map/ppermute | solution.py:20
  71.1 47.3 %copy-start.26 = (s32[2,32,16]{1,2,0:T(8,128)}, s32[2,32,16]{1,2,0:T(8,128)S(1)}, u32[]{:S(2)}) copy-start(s32[2,32,16]{1,2,0:T(8,128)S(1)} %iota_add_fusion.1) | copy-start | bytes 12292
  165.0 35.7 %collective-permute-start.3 = (f32[5,32,20,2]{1,3,2,0:T(2,128)}, f32[5,32,20,2]{1,3,2,0:T(2,128)}, u32[]{:S(2)}, u32[]{:S(2)}) collective-permute-start(f32[5,32,20,2]{1,3,2,0:T(2,128)} %copy.89), channel_id=1, source_target_pairs={{0,1},{1,2},{2,3},{3,4},{4,5},{5,6},{6,7},{8,9},{9,10},{10,11},{11... | collective-permute-start | bytes 76808 | tf_op jit(solution)/shard_map/ppermute | solution.py:20
  174.7 30.3 %collective-permute-start.2 = (f32[5,32,20,2]{1,3,2,0:T(2,128)}, f32[5,32,20,2]{1,3,2,0:T(2,128)}, u32[]{:S(2)}, u32[]{:S(2)}) collective-permute-start(f32[5,32,20,2]{1,3,2,0:T(2,128)} %copy.87), channel_id=1, source_target_pairs={{1,0},{2,1},{3,2},{4,3},{5,4},{6,5},{7,6},{9,8},{10,9},{11,10},{12... | collective-permute-start | bytes 76808 | tf_op jit(solution)/shard_map/ppermute | solution.py:22
  185.5 41.0 %collective-permute-start.11 = (f32[5,32,20,2]{1,3,2,0:T(2,128)}, f32[5,32,20,2]{1,3,2,0:T(2,128)}, u32[]{:S(2)}, u32[]{:S(2)}) collective-permute-start(f32[5,32,20,2]{1,3,2,0:T(2,128)} %copy.109), channel_id=1, source_target_pairs={{0,1},{1,2},{2,3},{3,4},{4,5},{5,6},{6,7},{8,9},{9,10},{10,11},{11... | collective-permute-start | bytes 76808 | tf_op jit(solution)/shard_map/ppermute | solution.py:20
  198.7 32.2 %collective-permute-start.10 = (f32[5,32,20,2]{1,3,2,0:T(2,128)}, f32[5,32,20,2]{1,3,2,0:T(2,128)}, u32[]{:S(2)}, u32[]{:S(2)}) collective-permute-start(f32[5,32,20,2]{1,3,2,0:T(2,128)} %copy.107), channel_id=1, source_target_pairs={{1,0},{2,1},{3,2},{4,3},{5,4},{6,5},{7,6},{9,8},{10,9},{11,10},{12... | collective-permute-start | bytes 76808 | tf_op jit(solution)/shard_map/ppermute | solution.py:22
  222.5 149.0 %collective-permute-start.5 = (f32[5,32,2,128]{3,0,2,1:T(8,128)}, f32[5,32,2,128]{3,0,2,1:T(8,128)}, u32[]{:S(2)}, u32[]{:S(2)}) collective-permute-start(f32[5,32,2,128]{3,0,2,1:T(8,128)} %get-tuple-element.40), channel_id=1, source_target_pairs={{0,8},{8,16},{16,24},{24,32},{32,40},{40,48},{48,56},{56,64},{64,7... | collective-permute-start | bytes 491528 | tf_op jit(solution)/shard_map/ppermute | solution.py:20
  224.6 146.9 %collective-permute-start.4 = (f32[5,32,2,128]{3,0,2,1:T(8,128)}, f32[5,32,2,128]{3,0,2,1:T(8,128)}, u32[]{:S(2)}, u32[]{:S(2)}) collective-permute-start(f32[5,32,2,128]{3,0,2,1:T(8,128)} %get-tuple-element.39), channel_id=1, source_target_pairs={{8,0},{16,8},{24,16},{32,24},{40,32},{48,40},{56,48},{64,56},{72,6... | collective-permute-start | bytes 491528 | tf_op jit(solution)/shard_map/ppermute | solution.py:22
  253.1 133.2 %collective-permute-start.13 = (f32[5,32,2,128]{3,0,2,1:T(8,128)}, f32[5,32,2,128]{3,0,2,1:T(8,128)S(1)}, u32[]{:S(2)}, u32[]{:S(2)}) collective-permute-start(f32[5,32,2,128]{3,0,2,1:T(8,128)} %get-tuple-element.36), channel_id=1, source_target_pairs={{0,8},{8,16},{16,24},{24,32},{32,40},{40,48},{48,56},{56,64},{64,7... | collective-permute-start | bytes 491528 | tf_op jit(solution)/shard_map/ppermute | solution.py:20
  256.1 130.2 %collective-permute-start.12 = (f32[5,32,2,128]{3,0,2,1:T(8,128)}, f32[5,32,2,128]{3,0,2,1:T(8,128)}, u32[]{:S(2)}, u32[]{:S(2)}) collective-permute-start(f32[5,32,2,128]{3,0,2,1:T(8,128)} %get-tuple-element.35), channel_id=1, source_target_pairs={{8,0},{16,8},{24,16},{32,24},{40,32},{48,40},{56,48},{64,56},{72,6... | collective-permute-start | bytes 491528 | tf_op jit(solution)/shard_map/ppermute | solution.py:22
  261.7 378.5 %all-reduce.5.cloned.1.call-start = ((), (), s32[]{:S(2)}) async-start(), calls=%async_computation | async-start | bytes 1310720
  265.4 106.1 %copy-start.4 = (f32[5,32,16,128]{3,0,2,1:T(8,128)S(1)}, f32[5,32,16,128]{3,0,2,1:T(8,128)}, u32[]{:S(2)}) copy-start(f32[5,32,16,128]{3,0,2,1:T(8,128)} %copy-done.3) | copy-start | bytes 3932164
  378.5 29.1 %collective-permute-start.7 = (f32[5,32,20,2]{1,3,2,0:T(2,128)}, f32[5,32,20,2]{1,3,2,0:T(2,128)}, u32[]{:S(2)}, u32[]{:S(2)}) collective-permute-start(f32[5,32,20,2]{1,3,2,0:T(2,128)} %copy.104), channel_id=1, source_target_pairs={{0,1},{1,2},{2,3},{3,4},{4,5},{5,6},{6,7},{8,9},{9,10},{10,11},{11... | collective-permute-start | bytes 76808 | tf_op jit(solution)/shard_map/ppermute | solution.py:20
  384.3 27.5 %collective-permute-start.6 = (f32[5,32,20,2]{1,3,2,0:T(2,128)}, f32[5,32,20,2]{1,3,2,0:T(2,128)}, u32[]{:S(2)}, u32[]{:S(2)}) collective-permute-start(f32[5,32,20,2]{1,3,2,0:T(2,128)} %copy.102), channel_id=1, source_target_pairs={{1,0},{2,1},{3,2},{4,3},{5,4},{6,5},{7,6},{9,8},{10,9},{11,10},{12... | collective-permute-start | bytes 76808 | tf_op jit(solution)/shard_map/ppermute | solution.py:22
  393.4 34.0 %collective-permute-start.15 = (f32[5,32,20,2]{1,3,2,0:T(2,128)S(1)}, f32[5,32,20,2]{1,3,2,0:T(2,128)}, u32[]{:S(2)}, u32[]{:S(2)}) collective-permute-start(f32[5,32,20,2]{1,3,2,0:T(2,128)S(1)} %copy.114), channel_id=1, source_target_pairs={{0,1},{1,2},{2,3},{3,4},{4,5},{5,6},{6,7},{8,9},{9,10},{10,11},{11... | collective-permute-start | bytes 76808 | tf_op jit(solution)/shard_map/ppermute | solution.py:20
  405.1 11.1 %copy-start.21 = (f32[5,32,128]{2,0,1:T(8,128)S(1)}, f32[5,32,128]{2,0,1:T(8,128)}, u32[]{:S(2)}) copy-start(f32[5,32,128]{2,0,1:T(8,128)} %copy.97) | copy-start | bytes 245764
  405.2 26.6 %collective-permute-start.14 = (f32[5,32,20,2]{1,3,2,0:T(2,128)}, f32[5,32,20,2]{1,3,2,0:T(2,128)}, u32[]{:S(2)}, u32[]{:S(2)}) collective-permute-start(f32[5,32,20,2]{1,3,2,0:T(2,128)} %copy.112), channel_id=1, source_target_pairs={{1,0},{2,1},{3,2},{4,3},{5,4},{6,5},{7,6},{9,8},{10,9},{11,10},{12... | collective-permute-start | bytes 76808 | tf_op jit(solution)/shard_map/ppermute | solution.py:22
  (33 other events, 249.7 us)
Sparse Core Ops, SparseCore 0:
  261.8 108.1 all-reduce.6
  372.6 267.4 all-reduce.4
where the time goes:
time: 658 us; the launch traced here: 649 us
  waiting for transfers between devices  296 us (45%)
  local copies, waits for them, and re-layouts  107 us (16%)
  blocking collectives  92.3 us (14%)
  matrix products  70.2 us (11%)
  starting transfers between devices  56.7 us (9%)
  between operations  16.8 us (3%)
  other arithmetic  9.72 us (1%)
    unnamed x4, waiting for transfers between devices  296 us
    all_gather x1, blocking collectives, body(): lax.all_gather(parent_we, 'gx', axis=2, tiled=True)  46.6 us
    all_gather x1, blocking collectives, body(): lax.all_gather(parent_sn, 'gy', axis=2, tiled=True)  45.7 us
    ppermute x8, starting transfers between devices, with_halo(): lax.ppermute(tail, axis, [(i, (i + 1) % count) for i in range(ends)])  42.4 us
    dot_general x2, matrix products, mix_back(): return jnp.einsum('gf,gkxy->fkxy', field_mix, values, precision=highest)  26.3 us
    slice x12, local copies, waits for them, and re-layouts, with_halo(): head = lax.slice_in_dim(cells, 0, width, axis=dim)  25.4 us
    dot_general x2, matrix products, mix_ahead(): return jnp.einsum('fg,gkxy->fkxy', field_mix, values, precision=highest)  22.1 us
    dot_general x2, matrix products, fold_with(): return jnp.einsum('eflc,eklc->efkc', section, weights, precision=highest)  17.8 us
  transfers between devices with their start and end apart: 18, of which 2 were waited for; matrix products, arithmetic and copies ran while one was open for 28% of the time, Pallas kernels for 0%

commit v1 on v0

v1 whole, which is shorter than its diff:
```python
import functools

import jax
import jax.numpy as jnp
from jax import lax
from jax.experimental import pallas as pl
from jax.experimental.pallas import tpu as pltpu
from jax.sharding import PartitionSpec as P

MESH = pl.DeviceIdType.MESH
F, KC, KP, CX, CY = 5, 32, 128, 16, 128
G = KC // 8
f32 = jnp.float32

L_COT, L_DIF, L_STATE, L_TWE, L_TSN, L_PWE, L_PSN, L_GWE, L_GSN, L_GRAD, L_FINAL, L_MIX, L_RW = range(13)
R_Q1, R_U0, R_Q2, R_U1 = range(4)
LEFT, RIGHT, DOWN, UP = range(4)
S_PWE, S_PSN = 16, 18
S_GWE, S_GSN = 20, 22
NSEM = 24


def tile(shape_dim):
    return lax.broadcasted_iota(jnp.int32, (8, CY), shape_dim)


def kernel(
    nx, ny,
    state, cot, dif, mix_in, pwe_in, psn_in, twe_in, tsn_in, rw_in,
    final, grad, gwe, gsn,
    u0, u1, q1, q2, a0, mid, out_f, out_g, edge, dp, dz, ztab,
    pwe, psn, bwe, bsn, gw, gs, packs, heard, own, halo, twe, tsn, mix, rw,
    loc, snd, rcv,
):
    gx, gy = lax.axis_index("gx"), lax.axis_index("gy")
    lane = tile(1)
    low2, high2, quad = lane < 2, lane >= CY - 2, lax.rem(lane, 4) < 2
    ends2 = low2 | high2
    x_end, y_end = (gx == 0) | (gx == nx - 1), (gy == 0) | (gy == ny - 1)

    def here(src, dst, sem):
        return pltpu.make_async_copy(src, dst, loc.at[sem])

    def whole(ref, sems, i):
        return pltpu.make_async_copy(ref, ref, sems.at[i])

    for x in range(CX):
        here(cot.at[:, :, x, :], a0.at[:, x], L_COT).start()
        here(dif.at[:, x, :], dp.at[x], L_DIF).start()
    here(twe_in, twe, L_TWE).start()
    here(tsn_in, tsn, L_TSN).start()
    here(mix_in, mix, L_MIX).start()
    here(rw_in, rw, L_RW).start()
    for x in range(CX):
        here(state.at[:, :, x, :], u0.at[:, x + 2], L_STATE).start()

    barrier = pltpu.get_barrier_semaphore()

    def greet(cond, to):
        @pl.when(cond)
        def _():
            pl.semaphore_signal(barrier, inc=1, device_id=to, device_id_type=MESH)

    def count(*conds):
        return sum(c.astype(jnp.int32) for c in conds)

    near = [(gx > 0, {"gx": gx - 1}), (gx < nx - 1, {"gx": gx + 1}), (gy > 0, {"gy": gy - 1}), (gy < ny - 1, {"gy": gy + 1})]
    for cond, to in near:
        greet(cond, to)
    for axis, at, n in (("gx", gx, nx), ("gy", gy, ny)):
        for e in (0, n - 1):
            @pl.when(at == e)
            def _(axis=axis, e=e, n=n):
                def one(i, c):
                    to = i + 1 if e == 0 else i
                    pl.semaphore_signal(barrier, inc=1, device_id={axis: to}, device_id_type=MESH)
                    return c
                lax.fori_loop(0, n - 1, one, 0)
            greet(at != e, {axis: jnp.int32(e)})
    wanted = count(*[c for c, _ in near])
    for at, n in ((gx, nx), (gy, ny)):
        for e in (0, n - 1):
            wanted = wanted + jnp.where(at == e, n - 1, 1)
    pl.semaphore_wait(barrier, wanted)

    def send(src, dst, i, j, to):
        return pltpu.make_async_remote_copy(src_ref=src, dst_ref=dst, send_sem=snd.at[i], recv_sem=rcv.at[j], device_id=to, device_id_type=MESH)

    @pl.when(gx > 0)
    def _():
        for i in range(2):
            send(state.at[:, :, i, :], u0.at[:, CX + 2 + i], 4 * R_U0 + LEFT, 4 * R_U0 + LEFT, {"gx": gx - 1}).start()

    @pl.when(gx < nx - 1)
    def _():
        for i in range(2):
            send(state.at[:, :, CX - 2 + i, :], u0.at[:, i], 4 * R_U0 + RIGHT, 4 * R_U0 + RIGHT, {"gx": gx + 1}).start()

    gather = (("gx", gx, nx, pwe_in, pwe, S_PWE, L_PWE), ("gy", gy, ny, psn_in, psn, S_PSN, L_PSN))
    for axis, at, n, src, dst, s, l in gather:
        for e, end in ((0, 0), (1, n - 1)):
            @pl.when(at != end)
            def _():
                send(src.at[e], dst.at[at], s + e, s, {axis: jnp.int32(end)}).start()

            @pl.when(at == end)
            def _():
                here(src.at[e], dst.at[end], l).start()

    zero = jnp.zeros((8, CY), f32)

    def clear(cond, ref, cols):
        @pl.when(cond)
        def _():
            for c in cols:
                for b in ref:
                    b[:, c] = jnp.zeros((F, KC, CY), f32)

    clear(gx == 0, (u0, u1, q1, q2), (0, 1))
    clear(gx == nx - 1, (u0, u1, q1, q2), (CX + 2, CX + 3))

    @pl.when(gy == 0)
    def _():
        heard[:, 0] = jnp.zeros((4, 5, 8, CY), f32)

    @pl.when(gy == ny - 1)
    def _():
        heard[:, 1] = jnp.zeros((4, 5, 8, CY), f32)

    here(rw_in, rw, L_RW).wait()
    width = jnp.full((8, CY), rw[0], jnp.int32)
    scale = (width + 1).astype(f32)
    pos_y = gy * CY + lane
    wy = jnp.maximum(width - jnp.minimum(pos_y, ny * CY - 1 - pos_y), 0).astype(f32) / scale

    def wx_of(x):
        pos = gx * CX + x
        return jnp.maximum(width - jnp.minimum(pos, nx * CX - 1 - pos), 0).astype(f32) / scale

    def weights(x, c):
        ztab[x] = (1.0 - wx_of(x)) * (1.0 - wy)
        return c

    lax.fori_loop(0, CX, weights, 0)

    def rows(g):
        return pl.ds(8 * g, 8)

    def slot(x, f, g):
        if f < 4:
            return g, f // 2, 8 * x + 4 * (f % 2) + 2 * (f // 2)
        return 4, g // 2, 8 * x + 4 * (g % 2) + 2 * (g // 2)

    def put(acc, v, x, f, g):
        i, fam, p = slot(x, f, g)
        moved = pltpu.roll(jnp.where(ends2, v, 0.0), lax.rem(p + 2, CY), 1)
        acc[2 * i + fam] = acc[2 * i + fam] + moved

    def ship_y(r, acc):
        for i in range(10):
            own[r, i] = acc[i]
        for i in range(5):
            packs[r, 1, i] = jnp.where(quad, acc[2 * i], acc[2 * i + 1])
            packs[r, 0, i] = jnp.where(quad, acc[2 * i + 1], acc[2 * i])

        @pl.when(gy > 0)
        def _():
            send(packs.at[r, 0], heard.at[r, 1], 4 * r + DOWN, 4 * r + DOWN, {"gy": gy - 1}).start()

        @pl.when(gy < ny - 1)
        def _():
            send(packs.at[r, 1], heard.at[r, 0], 4 * r + UP, 4 * r + UP, {"gy": gy + 1}).start()

    def ship_x(r, ref):
        @pl.when(gx > 0)
        def _():
            send(ref.at[:, 2:4], ref.at[:, CX + 2 : CX + 4], 4 * r + LEFT, 4 * r + LEFT, {"gx": gx - 1}).start()

        @pl.when(gx < nx - 1)
        def _():
            send(ref.at[:, CX : CX + 2], ref.at[:, 0:2], 4 * r + RIGHT, 4 * r + RIGHT, {"gx": gx + 1}).start()

    def await_x(r, ref):
        @pl.when(gx > 0)
        def _():
            whole(ref.at[:, 0:2], rcv, 4 * r + RIGHT).wait()

        @pl.when(gx < nx - 1)
        def _():
            whole(ref.at[:, CX + 2 : CX + 4], rcv, 4 * r + LEFT).wait()

    def await_y(r):
        @pl.when(gy > 0)
        def _():
            whole(heard.at[r, 0], rcv, 4 * r + UP).wait()

        @pl.when(gy < ny - 1)
        def _():
            whole(heard.at[r, 1], rcv, 4 * r + DOWN).wait()

        for i in range(5):
            lo, hi = heard[r, 0, i], heard[r, 1, i]
            for fam in range(2):
                d = (jnp.where(quad, hi, lo) if fam else jnp.where(quad, lo, hi)) - own[r, 2 * i + fam]
                place = lax.rem(lane + 2 * fam, 4)
                near = jnp.where(place == 1, pltpu.roll(d, CY - 1, 1), jnp.where(place == 2, pltpu.roll(d, 1, 1), 0.0))
                far = jnp.where(place < 2, pltpu.roll(d, CY - 2, 1), pltpu.roll(d, 2, 1))
                halo[2 * i + fam] = near - 0.0625 * far

    def lap(ref, x, f, g):
        i, fam, p = slot(x, f, g)
        mend = jnp.where(ends2, pltpu.roll(halo[2 * i + fam], (CY - 2) - p, 1), 0.0)
        c = ref[f, x + 2, rows(g)]
        s1 = pltpu.roll(c, 1, 1) + pltpu.roll(c, CY - 1, 1)
        s2 = pltpu.roll(c, 2, 1) + pltpu.roll(c, CY - 2, 1)
        s1 = s1 + (ref[f, x + 1, rows(g)] + ref[f, x + 3, rows(g)])
        s2 = s2 + (ref[f, x, rows(g)] + ref[f, x + 4, rows(g)])
        return (s1 + mend) - 0.0625 * s2 - 3.75 * c, c

    none = tuple(zero for _ in range(10))

    here(mix_in, mix, L_MIX).wait()
    whole(dp, loc, L_DIF).wait()
    whole(a0, loc, L_COT).wait()

    def first(x, acc):
        acc = list(acc)
        z = ztab[x]
        for g in range(G):
            d = dp[x, rows(g)] * (4.0 / 3.0)
            dp[x, rows(g)] = d
            w = d * z
            dz[x, rows(g)] = w
            for f in range(F):
                v = w * a0[f, x, rows(g)]
                q1[f, x + 2, rows(g)] = v
                put(acc, v, x, f, g)
        return tuple(acc)

    ship = lax.fori_loop(0, CX, first, none)
    ship_x(R_Q1, q1)
    ship_y(R_Q1, ship)

    whole(u0.at[:, 2 : CX + 2], loc, L_STATE).wait()

    def second(x, acc):
        acc = list(acc)
        for g in range(G):
            for f in range(F):
                put(acc, u0[f, x + 2, rows(g)], x, f, g)
        return tuple(acc)

    ship_y(R_U0, lax.fori_loop(0, CX, second, none))

    taps = [[mix[a, b] * 0.25 + (1.0 if a == b else 0.0) for b in range(F)] for a in range(F)]

    def blend(v, f, back):
        total = (taps[0][f] if back else taps[f][0]) * v[0]
        for g in range(1, F):
            total = total + (taps[g][f] if back else taps[f][g]) * v[g]
        return total

    def retreat(src, q, dst, nxt, x, acc):
        acc = list(acc)
        z = ztab[x]
        for g in range(G):
            p = [z * src[f, x, rows(g)] for f in range(F)]
            for f in range(F):
                t, _ = lap(q, x, f, g)
                m = t + blend(p, f, True)
                dst[f, x, rows(g)] = m
                if nxt is not None:
                    v = dz[x, rows(g)] * m
                    nxt[f, x + 2, rows(g)] = v
                    put(acc, v, x, f, g)
        return tuple(acc)

    def advance(u, dst, shift, pack, x, acc):
        acc = list(acc)
        z = ztab[x]
        for g in range(G):
            d = dp[x, rows(g)]
            both = [lap(u, x, f, g) for f in range(F)]
            c = [b[1] for b in both]
            for f in range(F):
                v = z * (d * both[f][0] + blend(c, f, False)) + edge[f, x, rows(g)]
                dst[f, x + shift, rows(g)] = v
                if pack:
                    put(acc, v, x, f, g)
        return tuple(acc)

    def sweep(r, ref, step):
        await_y(r)
        acc = lax.fori_loop(2, CX - 2, step, none)
        await_x(r, ref)
        return lax.fori_loop(0, 4, lambda i, a: step(i + (i // 2) * (CX - 4), a), acc)

    acc = sweep(R_Q1, q1, functools.partial(retreat, a0, q1, mid, q2))
    ship_x(R_Q2, q2)
    ship_y(R_Q2, acc)

    here(twe_in, twe, L_TWE).wait()
    here(tsn_in, tsn, L_TSN).wait()

    def climb(d, t, width_of):
        arr = jnp.concatenate([d, jnp.zeros((8, width_of), f32)], 0)
        for b in (1, 2, 4):
            arr = jnp.where((t & b)[0:1] != 0, pltpu.roll(arr, b, 0), arr)
        tiles = [arr[8 * j : 8 * j + 8] for j in range(5)]
        for b, size in ((8, 6), (16, 8), (32, 12), (64, 16)):
            on, gap = (t & b) != 0, b // 8
            blank = jnp.zeros((8, width_of), f32)
            take = lambda j: tiles[j] if 0 <= j < len(tiles) else blank
            tiles = [jnp.where(on, take(j - gap), take(j)) for j in range(size)]
        return tiles

    def descend(tiles, t):
        for b, size in ((64, 12), (32, 8), (16, 6), (8, 5)):
            on, gap = (t & b) != 0, b // 8
            tiles = [jnp.where(on, tiles[j + gap], tiles[j]) if j + gap < len(tiles) else tiles[j] for j in range(size)]
        arr = jnp.concatenate(tiles, 0)
        for b in (4, 2, 1):
            arr = jnp.where((t & b)[0:1] != 0, pltpu.roll(arr, 40 - b, 0), arr)
        return arr[0:KC]

    t_we = jnp.broadcast_to(jnp.where(gx == 0, twe[0:1], twe[1:2]), (8, CY))
    t_sn = jnp.broadcast_to(jnp.where(gy == 0, tsn[0:1], tsn[1:2]), (8, CX))

    @pl.when(x_end)
    def _():
        def one(f, c):
            def add(x, s):
                return s + jnp.tile((1.0 - wy) * wx_of(x), (G, 1)) * (a0[f, x] + mid[f, x])

            tiles = climb(lax.fori_loop(0, CX, add, jnp.zeros((KC, CY), f32)), t_we, CY)
            for j in range(16):
                gw[2 * j, f] = tiles[j][0:4]
                gw[2 * j + 1, f] = tiles[j][4:8]
            return c

        lax.fori_loop(0, F, one, 0)

    @pl.when(y_end)
    def _():
        def one(f, c):
            col = lax.broadcasted_iota(jnp.int32, (KC, CX), 1)

            def add(x, s):
                v = jnp.sum(jnp.tile(wy, (G, 1)) * (a0[f, x] + mid[f, x]), axis=1, keepdims=True)
                return jnp.where(col == x, v, s)

            tiles = climb(lax.fori_loop(0, CX, add, jnp.zeros((KC, CX), f32)), t_sn, CX)
            for j in range(16):
                gs[j // 2, f, 8 * (j % 2) : 8 * (j % 2) + 8] = tiles[j]
            return c

        lax.fori_loop(0, F, one, 0)

    spread = (("gx", gx, nx, gw, gwe, S_GWE, L_GWE), ("gy", gy, ny, gs, gsn, S_GSN, L_GSN))
    for axis, at, n, src, dst, s, l in spread:
        for e, end in ((0, 0), (1, n - 1)):
            @pl.when(at == end)
            def _():
                here(src.at[end], dst.at[e], l).start()

                def one(i, c):
                    to = i + 1 if e == 0 else i
                    send(src.at[to], dst.at[e], s, s + e, {axis: to}).start()
                    return c

                lax.fori_loop(0, n - 1, one, 0)

    for axis, at, n, src, dst, s, l in gather:
        for e, end in ((0, 0), (1, n - 1)):
            @pl.when(at == end)
            def _():
                rest = dst.at[1:n] if e == 0 else dst.at[0 : n - 1]
                whole(rest, rcv, s).wait()
                here(src.at[e], dst.at[end], l).wait()

    @pl.when(x_end)
    def _():
        def one(f, c):
            tiles = [jnp.concatenate([pwe[2 * j, f], pwe[2 * j + 1, f]], 0) for j in range(16)]
            bwe[f] = descend(tiles, t_we)
            return c

        lax.fori_loop(0, F, one, 0)

    @pl.when(jnp.logical_not(x_end))
    def _():
        bwe[...] = jnp.zeros((F, KC, CY), f32)

    @pl.when(y_end)
    def _():
        def one(f, c):
            tiles = [psn[j // 2, f, 8 * (j % 2) : 8 * (j % 2) + 8] for j in range(16)]
            bsn[f] = descend(tiles, t_sn)
            return c

        lax.fori_loop(0, F, one, 0)

    @pl.when(jnp.logical_not(y_end))
    def _():
        bsn[...] = jnp.zeros((F, KC, CX), f32)

    @pl.when(x_end | y_end)
    def _():
        def one(f, c):
            b = bsn[f]
            for x in range(CX):
                w = jnp.tile((1.0 - wy) * wx_of(x), (G, 1))
                edge[f, x] = w * bwe[f] + jnp.tile(wy, (G, 1)) * b[:, x : x + 1]
            return c

        lax.fori_loop(0, F, one, 0)

    @pl.when(jnp.logical_not(x_end | y_end))
    def _():
        def one(x, c):
            edge[:, x] = jnp.zeros((F, KC, CY), f32)
            return c

        lax.fori_loop(0, CX, one, 0)

    acc = sweep(R_U0, u0, functools.partial(advance, u0, u1, 2, True))
    ship_x(R_U1, u1)
    ship_y(R_U1, acc)

    sweep(R_Q2, q2, functools.partial(retreat, mid, q2, out_g, None))
    for x in range(CX):
        here(out_g.at[:, x], grad.at[:, :, x, :], L_GRAD).start()

    sweep(R_U1, u1, functools.partial(advance, u1, out_f, 0, False))
    for x in range(CX):
        here(out_f.at[:, x], final.at[:, :, x, :], L_FINAL).start()

    for r, ref in ((R_Q1, q1), (R_U0, u0), (R_Q2, q2), (R_U1, u1)):
        pair = ref.at[:, 0:2]
        for way, cond, what in (
            (LEFT, gx > 0, pair), (RIGHT, gx < nx - 1, pair),
            (DOWN, gy > 0, packs.at[r, 0]), (UP, gy < ny - 1, packs.at[r, 1]),
        ):
            @pl.when(cond)
            def _():
                whole(what, snd, 4 * r + way).wait()

    for axis, at, n, src, dst, s, l in gather:
        for e, end in ((0, 0), (1, n - 1)):
            @pl.when(at != end)
            def _():
                whole(src.at[e], snd, s + e).wait()

    for axis, at, n, src, dst, s, l in spread:
        for e, end in ((0, 0), (1, n - 1)):
            @pl.when(at == end)
            def _():
                whole(src.at[1:n] if e == 0 else src.at[0 : n - 1], snd, s).wait()
                here(src.at[end], dst.at[e], l).wait()

            @pl.when(at != end)
            def _():
                whole(dst.at[e], rcv, s + e).wait()

    whole(out_g, loc, L_GRAD).wait()
    whole(out_f, loc, L_FINAL).wait()


def solution(mesh):
    nx, ny = mesh.shape["gx"], mesh.shape["gy"]
    wide, flat = (F, CX + 4, KC, CY), (F, CX, KC, CY)

    def body(*args):
        anywhere = pl.BlockSpec(memory_space=pl.ANY)
        scratch = [wide] * 4 + [flat] * 5 + [
            (CX, KC, CY), (CX, KC, CY), (CX, 8, CY),
            (nx, F, KP // nx, CY), (ny, F, KP // ny, CX), (F, KC, CY), (F, KC, CX),
            (nx, F, KP // nx, CY), (ny, F, KP // ny, CX),
            (4, 2, 5, 8, CY), (4, 2, 5, 8, CY), (4, 10, 8, CY), (10, 8, CY),
        ]
        child = jax.ShapeDtypeStruct((F, KC, CX, CY), f32)
        return pl.pallas_call(
            functools.partial(kernel, nx, ny),
            out_shape=(
                child, child,
                jax.ShapeDtypeStruct((2, F, KP // nx, CY), f32),
                jax.ShapeDtypeStruct((2, F, KP // ny, CX), f32),
            ),
            in_specs=[anywhere] * 9,
            out_specs=[anywhere] * 4,
            scratch_shapes=[pltpu.VMEM(s, f32) for s in scratch] + [
                pltpu.VMEM((2, CY), jnp.int32),
                pltpu.VMEM((2, CX), jnp.int32),
                pltpu.SMEM((F, F), f32),
                pltpu.SMEM((1,), jnp.int32),
                pltpu.SemaphoreType.DMA((13,)),
                pltpu.SemaphoreType.DMA((NSEM,)),
                pltpu.SemaphoreType.DMA((NSEM,)),
            ],
            compiler_params=pltpu.CompilerParams(
                collective_id=0, has_side_effects=True, vmem_limit_bytes=56 * 2**20
            ),
            name="nest",
        )(*args)

    return jax.shard_map(
        body,
        mesh=mesh,
        in_specs=(
            P(None, None, "gx", "gy"),
            P(None, None, "gx", "gy"),
            P(None, "gx", "gy"),
            P(),
            P(None, None, "gx", "gy"),
            P(None, None, "gy", "gx"),
            P(None, "gy"),
            P(None, "gx"),
            P(),
        ),
        out_specs=(
            P(None, None, "gx", "gy"),
            P(None, None, "gx", "gy"),
            P(None, None, "gx", "gy"),
            P(None, None, "gy", "gx"),
        ),
        check_vma=False,
    )
```

time: 658 us -> 47.2 us (0.07); the launches traced: 649 us -> 47.1 us
  waiting for transfers between devices: 296 us -> 0 us
  local copies, waits for them, and re-layouts: 107 us -> 4.92 us
  blocking collectives: 92.3 us -> 0 us
  matrix products: 70.2 us -> 0 us
  starting transfers between devices: 56.7 us -> 0 us
  Pallas kernels: 0 us -> 40.8 us
  between operations: 16.8 us -> 1.3 us
  other arithmetic: 9.72 us -> 0 us
    unnamed x4 -> x0, waiting for transfers between devices: 296 us -> none
    all_gather x2 -> x0, blocking collectives: 92.3 us -> none  [the longest x1 46.6 us: body(): lax.all_gather(parent_we, 'gx', axis=2, tiled=True)]
    dot_general x8 -> x0, matrix products: 70.2 us -> none  [the longest x2 26.3 us: mix_back(): return jnp.einsum('gf,gkxy->fkxy', field_mix, values, precision=highest)]
    ppermute x16 -> x0, starting transfers between devices: 56.6 us -> none  [the longest x8 42.4 us: with_halo(): lax.ppermute(tail, axis, [(i, (i + 1) % count) for i in range(ends)])]
    pallas_call x0 -> x1, Pallas kernels: none -> 40.8 us  [body(): pl.pallas_call(functools.partial(kernel, nx, ny), out_shape=(child, child...]
    slice x16 -> x0, local copies, waits for them, and re-layouts: 37.6 us -> none  [the longest x12 25.4 us: with_halo(): head = lax.slice_in_dim(cells, 0, width, axis=dim)]
    ppermute x8 -> x0, local copies, waits for them, and re-layouts: 34.5 us -> none  [the longest x4 17.3 us: with_halo(): lax.ppermute(head, axis, [((i + 1) % count, i) for i in range(ends)])]
    unnamed x92 -> x10, local copies, waits for them, and re-layouts: 16.5 us -> 4.92 us
  transfers between devices with their start and end apart: 18 -> 0, of which waited for: 2 -> 0; matrix products, arithmetic and copies ran while one was open for 28% -> 0% of each run, Pallas kernels for 0% -> 0%
where the time goes in v1:
time: 47.2 us; the launch traced here: 47.1 us
  Pallas kernels  40.8 us (86%)
  local copies, waits for them, and re-layouts  4.92 us (10%)
  between operations  1.3 us (3%)
    pallas_call x1, Pallas kernels, body(): pl.pallas_call(functools.partial(kernel, nx, ny), out_shape=(child, child...  40.8 us
    unnamed x10, local copies, waits for them, and re-layouts  4.92 us

profile of v1, /device:TPU:6, one launch (start us, length us, event | category | flops | bytes accessed | tf_op | source)
XLA Modules:
  0.0 47.1 jit_solution(5006922836343382820)
XLA Ops:
  1.3 40.8 %nest.1 = (f32[5,32,16,128]{3,2,1,0:T(8,128)}, f32[5,32,16,128]{3,2,1,0:T(8,128)}, f32[2,5,4,128]{3,2,1,0:T(4,128)}, f32[2,5,16,16]{3,2,1,0:T(8,128)}) custom-call(f32[5,32,16,128]{3,2,1,0:T(8,128)} %state.1, f32[5,32,16,128]{3,2,1,0:T(8,128)} %cot.1, f32[32,16,128]{2,1,0:T(8,128)} %dif.1, f32[5,5]{1,0:T(8,128)} %mix_in.1, f32[2,5,4,128]{3,2,1,0:T(4,128)} %pwe_in.1, ...), custom_call_target="tpu_custom_call" | custom-call | tf_op jit(solution)/shard_map/nest/pallas_call | solution.py:482
  42.1 0.0 copy-start
  42.1 2.6 %copy.18 = f32[5,32,16,128]{3,2,1,0:T(8,128)} copy(f32[5,32,16,128]{3,2,1,0:T(8,128)} %get-tuple-element.8) | data formatting | bytes 2621440
  44.7 0.0 copy-done
  44.7 0.0 copy-start.2
  44.7 0.0 copy-start.1
  44.7 1.1 %copy.19 = f32[5,32,16,128]{3,2,1,0:T(8,128)} copy(f32[5,32,16,128]{3,2,1,0:T(8,128)S(1)} %copy-done) | data formatting | bytes 2621440
  45.8 0.0 copy-done.2
  45.8 0.6 %copy.20 = f32[2,5,4,128]{3,2,1,0:T(4,128)} copy(f32[2,5,4,128]{3,2,1,0:T(4,128)S(1)} %copy-done.2) | data formatting | bytes 40960
  46.4 0.0 copy-done.1
  46.4 0.6 %copy.21 = f32[2,5,16,16]{3,2,1,0:T(8,128)} copy(f32[2,5,16,16]{3,2,1,0:T(8,128)S(1)} %copy-done.1) | data formatting | bytes 20480
Async XLA Ops:
  42.1 2.6 %copy-start = (f32[5,32,16,128]{3,2,1,0:T(8,128)S(1)}, f32[5,32,16,128]{3,2,1,0:T(8,128)}, u32[]{:S(2)}) copy-start(f32[5,32,16,128]{3,2,1,0:T(8,128)} %get-tuple-element.9) | copy-start | bytes 3932164
  44.7 1.1 %copy-start.2 = (f32[2,5,4,128]{3,2,1,0:T(4,128)S(1)}, f32[2,5,4,128]{3,2,1,0:T(4,128)}, u32[]{:S(2)}) copy-start(f32[2,5,4,128]{3,2,1,0:T(4,128)} %get-tuple-element.10) | copy-start | bytes 61444
  44.7 1.7 %copy-start.1 = (f32[2,5,16,16]{3,2,1,0:T(8,128)S(1)}, f32[2,5,16,16]{3,2,1,0:T(8,128)}, u32[]{:S(2)}) copy-start(f32[2,5,16,16]{3,2,1,0:T(8,128)} %get-tuple-element.11) | copy-start | bytes 30724

commit v2 on v1

v2 whole, which is shorter than its diff:
```python
import functools

import jax
import jax.numpy as jnp
from jax import lax
from jax.experimental import pallas as pl
from jax.experimental.pallas import tpu as pltpu
from jax.sharding import PartitionSpec as P

MESH = pl.DeviceIdType.MESH
F, KC, KP, CX, CY = 5, 32, 128, 16, 128
G = KC // 8
f32 = jnp.float32

L_COT, L_DIF, L_STATE, L_TWE, L_TSN, L_PWE, L_PSN, L_GWE, L_GSN, L_MIX, L_RW, L_GRAD, L_FINAL = range(13)
R_Q1, R_U0, R_Q2, R_U1 = range(4)
LEFT, RIGHT, DOWN, UP = range(4)
S_PWE, S_PSN, S_GWE, S_GSN = 16, 18, 20, 22
S_PWE2, S_GWE2 = 24, 25
NSEM = 26
VMEM_LIMIT = 56 * 2**20
W = 8


def tile(shape_dim):
    return lax.broadcasted_iota(jnp.int32, (8, CY), shape_dim)


def kernel(
    nx, ny,
    state, cot, dif, mix_in, pwe_in, psn_in, twe_in, tsn_in, rw_in,
    final, grad, gwe, gsn,
    u0, u1, q1, q2, a0, mid, out_f, out_g, edge, dp, dz, ztab, xtab,
    pwe, psn, bwe, bsn, gw, gs, packs, heard, own, halo, twe, tsn, mix, rw,
    loc, snd, rcv, above, opened, entered,
):
    gx, gy = lax.axis_index("gx"), lax.axis_index("gy")
    lane = tile(1)
    low2, high2, quad = lane < 2, lane >= CY - 2, lax.rem(lane, 4) < 2
    ends2 = low2 | high2
    x_end, y_end = (gx == 0) | (gx == nx - 1), (gy == 0) | (gy == ny - 1)

    def here(src, dst, sem):
        return pltpu.make_async_copy(src, dst, loc.at[sem])

    def whole(ref, sems, i):
        return pltpu.make_async_copy(ref, ref, sems.at[i])

    barrier = pltpu.get_barrier_semaphore()

    def greet(cond, to):
        @pl.when(cond)
        def _():
            pl.semaphore_signal(barrier, inc=1, device_id=to, device_id_type=MESH)

    base = gx // W * W
    subs = (base, base + W - 1)
    west, east = gx == subs[0], gx == subs[1]
    both = [(gx > 0, {"gx": gx - 1}), (gx < nx - 1, {"gx": gx + 1})]
    for e, sub in enumerate(subs):
        both.append((gx != sub, {"gx": sub}))
        for j in range(W - 1):
            both.append((gx == sub, {"gx": base + j + 1 - e}))
    told = [(gy < ny - 1, {"gy": gy + 1}), (gy < ny - 1, {"gy": jnp.int32(ny - 1)})]
    told += [(gy == 0, {"gy": jnp.int32(j)}) for j in range(1, ny)]
    told += [(gx == 0, {"gx": jnp.int32(j)}) for j in range(W, nx, W)]
    told += [(east & (gx < nx - 1), {"gx": jnp.int32(nx - 1)})]
    for cond, to in both + told:
        greet(cond, to)
    wanted = sum(cond.astype(jnp.int32) for cond, _ in both)
    wanted = wanted + jnp.where(gy > 0, 2, 0) + jnp.where(gy == ny - 1, ny - 1, 0)
    wanted = wanted + jnp.where(west & (gx > 0), 1, 0) + jnp.where(gx == nx - 1, nx // W - 1, 0)

    here(rw_in, rw, L_RW).start()
    for x in range(CX):
        here(cot.at[:, :, x, :], a0.at[:, x], L_COT).start()
        here(dif.at[:, x, :], dp.at[x], L_DIF).start()
    here(mix_in, mix, L_MIX).start()
    for x in range(CX):
        here(state.at[:, :, x, :], u0.at[:, x + 2], L_STATE).start()
    here(twe_in, twe, L_TWE).start()
    here(tsn_in, tsn, L_TSN).start()

    def send(src, dst, i, j, to):
        return pltpu.make_async_remote_copy(src_ref=src, dst_ref=dst, send_sem=snd.at[i], recv_sem=rcv.at[j], device_id=to, device_id_type=MESH)

    def clear(cond, ref, cols):
        @pl.when(cond)
        def _():
            for c in cols:
                for b in ref:
                    b[:, c] = jnp.zeros((F, KC, CY), f32)

    clear(gx == 0, (u0, u1, q1, q2), (0, 1))
    clear(gx == nx - 1, (u0, u1, q1, q2), (CX + 2, CX + 3))

    @pl.when(gy == 0)
    def _():
        heard[:, 0] = jnp.zeros((4, 5, 8, CY), f32)

    @pl.when(gy == ny - 1)
    def _():
        heard[:, 1] = jnp.zeros((4, 5, 8, CY), f32)

    here(rw_in, rw, L_RW).wait()
    width = jnp.broadcast_to(rw[...], (8, CY))
    scale = (width + 1).astype(f32)
    pos_y = gy * CY + lane
    wy = jnp.maximum(width - jnp.minimum(pos_y, ny * CY - 1 - pos_y), 0).astype(f32) / scale

    def wx_of(x):
        pos = gx * CX + x
        return jnp.maximum(width - jnp.minimum(pos, nx * CX - 1 - pos), 0).astype(f32) / scale

    def weights(x, c):
        wx = wx_of(x)
        ztab[x] = (1.0 - wx) * (1.0 - wy)
        xtab[x] = (1.0 - wy) * wx
        return c

    lax.fori_loop(0, CX, weights, 0)

    def rows(g):
        return pl.ds(pl.multiple_of(8 * g, 8), 8)

    def slot(x, f):
        return (0, 8 * x + 4 * f) if f < 2 else (1, 8 * x + 4 * (f - 2) + 2) if f < 4 else (2, 8 * x)

    def put(acc, v, x, f):
        i, p = slot(x, f)
        acc[i] = acc[i] + pltpu.roll(jnp.where(ends2, v, 0.0), (p + 2) % CY, 1)

    def own_of(r, i):
        if i < G:
            return own[r, i, 0], own[r, i, 1]
        return own[r, 0, 2] + pltpu.roll(own[r, 1, 2], 4, 1), pltpu.roll(own[r, 2, 2], 2, 1) + pltpu.roll(own[r, 3, 2], 6, 1)

    def ship_y(r):
        for i in range(5):
            one, two = own_of(r, i)
            packs[r, 1, i] = jnp.where(quad, one, two)
            packs[r, 0, i] = jnp.where(quad, two, one)

        @pl.when(gy > 0)
        def _():
            send(packs.at[r, 0], heard.at[r, 1], 4 * r + DOWN, 4 * r + DOWN, {"gy": gy - 1}).start()

        if r in (R_Q2, R_U1):
            ship_up(r, gy < ny - 1)

    def ship_up(r, cond):
        @pl.when(cond)
        def _():
            if r == R_Q1:
                pl.semaphore_wait(above, 1)
            send(packs.at[r, 1], heard.at[r, 0], 4 * r + UP, 4 * r + UP, {"gy": gy + 1}).start()

    def ship_x(r, ref):
        @pl.when(gx > 0)
        def _():
            send(ref.at[:, 2:4], ref.at[:, CX + 2 : CX + 4], 4 * r + LEFT, 4 * r + LEFT, {"gx": gx - 1}).start()

        @pl.when(gx < nx - 1)
        def _():
            send(ref.at[:, CX : CX + 2], ref.at[:, 0:2], 4 * r + RIGHT, 4 * r + RIGHT, {"gx": gx + 1}).start()

    def await_x(r, ref):
        @pl.when(gx > 0)
        def _():
            whole(ref.at[:, 0:2], rcv, 4 * r + RIGHT).wait()

        @pl.when(gx < nx - 1)
        def _():
            whole(ref.at[:, CX + 2 : CX + 4], rcv, 4 * r + LEFT).wait()

    def await_y(r):
        @pl.when(gy > 0)
        def _():
            whole(heard.at[r, 0], rcv, 4 * r + UP).wait()

        @pl.when(gy < ny - 1)
        def _():
            whole(heard.at[r, 1], rcv, 4 * r + DOWN).wait()

        for i in range(5):
            lo, hi = heard[r, 0, i], heard[r, 1, i]
            mends = []
            for fam, mine in enumerate(own_of(r, i)):
                d = (jnp.where(quad, hi, lo) if fam else jnp.where(quad, lo, hi)) - mine
                place = lax.rem(lane + 2 * fam, 4)
                near = jnp.where(place == 1, pltpu.roll(d, CY - 1, 1), jnp.where(place == 2, pltpu.roll(d, 1, 1), 0.0))
                far = jnp.where(place < 2, pltpu.roll(d, CY - 2, 1), pltpu.roll(d, 2, 1))
                mends.append(near - 0.0625 * far)
            if i < G:
                halo[i, 0], halo[i, 1] = mends
            else:
                halo[0, 2] = mends[0]
                halo[1, 2] = pltpu.roll(mends[0], CY - 4, 1)
                halo[2, 2] = pltpu.roll(mends[1], CY - 2, 1)
                halo[3, 2] = pltpu.roll(mends[1], CY - 6, 1)

    def mend(x, f, g):
        i, p = slot(x, f)
        return jnp.where(ends2, pltpu.roll(halo[g, i], (CY - 2) - p, 1), 0.0)

    def lap(ref, x, f, g):
        c = ref[f, x + 2, rows(g)]
        s1 = pltpu.roll(c, 1, 1) + pltpu.roll(c, CY - 1, 1)
        s2 = pltpu.roll(c, 2, 1) + pltpu.roll(c, CY - 2, 1)
        s1 = s1 + (ref[f, x + 1, rows(g)] + ref[f, x + 3, rows(g)])
        s2 = s2 + (ref[f, x, rows(g)] + ref[f, x + 4, rows(g)])
        return s1 - 0.0625 * s2 - 3.75 * c, c

    def per_group(cols, step):
        def one(g, c):
            for x in cols:
                step(x, g)
            return c

        lax.fori_loop(0, G, one, 0)

    def pack(r, value):
        def one(g, c):
            acc = [jnp.zeros((8, CY), f32) for _ in range(3)]
            for x in range(CX):
                for f in range(F):
                    put(acc, value(x, f, g), x, f)
            for i in range(3):
                own[r, g, i] = acc[i]
            return c

        lax.fori_loop(0, G, one, 0)

    pl.semaphore_wait(barrier, wanted)
    @pl.when(gx > 0)
    def _():
        for i in range(2):
            send(state.at[:, :, i, :], u0.at[:, CX + 2 + i], 4 * R_U0 + LEFT, 4 * R_U0 + LEFT, {"gx": gx - 1}).start()

    @pl.when(gx < nx - 1)
    def _():
        for i in range(2):
            send(state.at[:, :, CX - 2 + i, :], u0.at[:, i], 4 * R_U0 + RIGHT, 4 * R_U0 + RIGHT, {"gx": gx + 1}).start()

    def signal(sem, axis, to):
        pl.semaphore_signal(sem, inc=1, device_id={axis: jnp.int32(to)}, device_id_type=MESH)

    @pl.when(gy > 0)
    def _():
        signal(above, "gy", gy - 1)
        signal(entered.at[1], "gy", 0)
        send(psn_in.at[0], psn.at[gy], S_PSN, S_PSN, {"gy": jnp.int32(0)}).start()

    @pl.when(gy == ny - 1)
    def _():
        for i in range(ny - 1):
            signal(opened.at[1], "gy", i)

    @pl.when(west & (gx > 0))
    def _():
        signal(entered.at[0], "gx", 0)

    @pl.when(gx == nx - 1)
    def _():
        for i in range(W - 1, nx - 1, W):
            signal(opened.at[0], "gx", i)

    whole(dp, loc, L_DIF).wait()
    whole(a0, loc, L_COT).wait()

    def first(x, g):
        d = dp[x, rows(g)] * (4.0 / 3.0)
        dp[x, rows(g)] = d
        w = d * ztab[x]
        dz[x, rows(g)] = w
        for f in range(F):
            v = w * a0[f, x, rows(g)]
            q1[f, x + 2, rows(g)] = v

    per_group(range(CX), first)
    pack(R_Q1, lambda x, f, g: q1[f, x + 2, rows(g)])

    ship_x(R_Q1, q1)
    ship_y(R_Q1)
    for e, sub in enumerate(subs):
        @pl.when(gx != sub)
        def _():
            send(pwe_in.at[e], pwe.at[gx], S_PWE + e, S_PWE, {"gx": sub}).start()

        @pl.when(gx == sub)
        def _():
            here(pwe_in.at[e], pwe.at[gx], L_PWE).start()

        @pl.when(gy == e * (ny - 1))
        def _():
            here(psn_in.at[e], psn.at[gy], L_PSN).start()

    whole(u0.at[:, 2 : CX + 2], loc, L_STATE).wait()

    pack(R_U0, lambda x, f, g: u0[f, x + 2, rows(g)])
    ship_y(R_U0)

    here(mix_in, mix, L_MIX).wait()
    taps = [[mix[a, b] * 0.25 + (1.0 if a == b else 0.0) for b in range(F)] for a in range(F)]

    def blend(v, f, back):
        total = (taps[0][f] if back else taps[f][0]) * v[0]
        for g in range(1, F):
            total = total + (taps[g][f] if back else taps[f][g]) * v[g]
        return total

    def retreat(src, q, dst, x, g):
        z = ztab[x]
        p = [z * src[f, x, rows(g)] for f in range(F)]
        for f in range(F):
            t, _ = lap(q, x, f, g)
            dst[f, x, rows(g)] = t + blend(p, f, True)

    def advance(u, dst, shift, x, g):
        z, d = ztab[x], dp[x, rows(g)]
        both = [lap(u, x, f, g) for f in range(F)]
        c = [b[1] for b in both]
        for f in range(F):
            dst[f, x + shift, rows(g)] = z * (d * both[f][0] + blend(c, f, False))

    def sweep(r, ref, step, between=None):
        per_group(range(2, CX - 2), step)
        if between is not None:
            between()
        await_x(r, ref)
        per_group((0, 1, CX - 2, CX - 1), step)

    def block_to(root):
        block = pwe.at[pl.ds(base, W)]
        return send(block, block, S_PWE2, S_PWE2, {"gx": jnp.int32(root)})

    def take_columns():
        for e, sub in enumerate(subs):
            @pl.when(gx == sub)
            def _():
                whole(pwe.at[pl.ds(base + 1 - e, W - 1)], rcv, S_PWE).wait()
                here(pwe_in.at[e], pwe.at[gx], L_PWE).wait()

        @pl.when(west & (gx > 0))
        def _():
            block_to(0).start()

        @pl.when(east & (gx < nx - 1))
        def _():
            pl.semaphore_wait(opened.at[0], 1)
            block_to(nx - 1).start()

    sweep(R_U0, u0, functools.partial(advance, u0, u1, 2))

    middle = gy == ny // 2 - 1
    ship_up(R_Q1, (gy < ny - 1) & jnp.logical_not(middle))
    ship_up(R_U0, (gy < ny - 1) & jnp.logical_not(middle))

    sweep(R_Q1, q1, functools.partial(retreat, a0, q1, mid), take_columns)

    ship_up(R_Q1, middle)
    ship_up(R_U0, middle)
    await_y(R_Q1)

    def settle_middle(x, f, g):
        m = mid[f, x, rows(g)] + mend(x, f, g)
        mid[f, x, rows(g)] = m
        v = dz[x, rows(g)] * m
        q2[f, x + 2, rows(g)] = v
        return v

    pack(R_Q2, settle_middle)
    ship_x(R_Q2, q2)
    ship_y(R_Q2)
    here(twe_in, twe, L_TWE).wait()
    here(tsn_in, tsn, L_TSN).wait()

    def climb(d, t, width_of):
        arr = jnp.concatenate([d, jnp.zeros((8, width_of), f32)], 0)
        for b in (1, 2, 4):
            arr = jnp.where((t & b)[0:1] != 0, pltpu.roll(arr, b, 0), arr)
        tiles = [arr[8 * j : 8 * j + 8] for j in range(5)]
        for b, size in ((8, 6), (16, 8), (32, 12), (64, 16)):
            on, gap = (t & b) != 0, b // 8
            blank = jnp.zeros((8, width_of), f32)
            take = lambda j: tiles[j] if 0 <= j < len(tiles) else blank
            tiles = [jnp.where(on, take(j - gap), take(j)) for j in range(size)]
        return tiles

    def descend(tiles, t):
        for b, size in ((64, 12), (32, 8), (16, 6), (8, 5)):
            on, gap = (t & b) != 0, b // 8
            tiles = [jnp.where(on, tiles[j + gap], tiles[j]) if j + gap < len(tiles) else tiles[j] for j in range(size)]
        arr = jnp.concatenate(tiles, 0)
        for b in (4, 2, 1):
            arr = jnp.where((t & b)[0:1] != 0, pltpu.roll(arr, 40 - b, 0), arr)
        return arr[0:KC]

    t_we = jnp.broadcast_to(jnp.where(gx == 0, twe[0:1], twe[1:2]), (8, CY))
    t_sn = jnp.broadcast_to(jnp.where(gy == 0, tsn[0:1], tsn[1:2]), (8, CX))

    @pl.when(x_end)
    def _():
        def one(f, c):
            d = []
            for g in range(G):
                s = xtab[0] * (a0[f, 0, rows(g)] + mid[f, 0, rows(g)])
                for x in range(1, CX):
                    s = s + xtab[x] * (a0[f, x, rows(g)] + mid[f, x, rows(g)])
                d.append(s)
            tiles = climb(jnp.concatenate(d, 0), t_we, CY)
            for j in range(16):
                gw[2 * j, f] = tiles[j][0:4]
                gw[2 * j + 1, f] = tiles[j][4:8]
            return c

        lax.fori_loop(0, F, one, 0)

    @pl.when(y_end)
    def _():
        def one(f, c):
            col = lax.broadcasted_iota(jnp.int32, (8, CX), 1)
            d = []
            for g in range(G):
                s = jnp.zeros((8, CX), f32)
                for x in range(CX):
                    v = jnp.sum(wy * (a0[f, x, rows(g)] + mid[f, x, rows(g)]), axis=1, keepdims=True)
                    s = jnp.where(col == x, v, s)
                d.append(s)
            tiles = climb(jnp.concatenate(d, 0), t_sn, CX)
            for j in range(16):
                gs[j // 2, f, 8 * (j % 2) : 8 * (j % 2) + 8] = tiles[j]
            return c

        lax.fori_loop(0, F, one, 0)

    def spread_we(e):
        root = e * (nx - 1)
        for j in range(nx // W):
            if j != root // W:
                block = gw.at[pl.ds(j * W, W)]
                send(block, block, S_GWE2, S_GWE2, {"gx": jnp.int32(j * W + e * (W - 1))}).start()

    def spread_sn(e):
        root = e * (ny - 1)
        here(gs.at[root], gsn.at[e], L_GSN).start()
        for j in range(ny):
            if j != root:
                send(gs.at[j], gsn.at[e], S_GSN, S_GSN + e, {"gy": jnp.int32(j)}).start()

    for e in range(2):
        @pl.when(gx == e * (nx - 1))
        def _():
            if e == 0:
                pl.semaphore_wait(entered.at[0], nx // W - 1)
            spread_we(e)

        @pl.when(gy == e * (ny - 1))
        def _():
            if e == 0:
                pl.semaphore_wait(entered.at[1], ny - 1)
            spread_sn(e)

    def relay_gradients():
        for e, sub in enumerate(subs):
            @pl.when((gx == sub) & (gx != e * (nx - 1)))
            def _():
                whole(gw.at[pl.ds(base, W)], rcv, S_GWE2).wait()

            @pl.when(gx == sub)
            def _():
                here(gw.at[gx], gwe.at[e], L_GWE).start()
                for j in range(W - 1):
                    to = base + j + 1 - e
                    send(gw.at[to], gwe.at[e], S_GWE, S_GWE + e, {"gx": to}).start()
    @pl.when(gy < ny - 1)
    def _():
        pl.semaphore_wait(opened.at[1], 1)
        send(psn_in.at[1], psn.at[gy], S_PSN + 1, S_PSN + 1, {"gy": jnp.int32(ny - 1)}).start()

    for e in range(2):
        @pl.when(gx == e * (nx - 1))
        def _():
            whole(pwe.at[0 : nx - W] if e else pwe.at[W:nx], rcv, S_PWE2).wait()

        @pl.when(gy == e * (ny - 1))
        def _():
            whole(psn.at[0 : ny - 1] if e else psn.at[1:ny], rcv, S_PSN + e).wait()
            here(psn_in.at[e], psn.at[gy], L_PSN).wait()

    @pl.when(x_end)
    def _():
        def one(f, c):
            tiles = [jnp.concatenate([pwe[2 * j, f], pwe[2 * j + 1, f]], 0) for j in range(16)]
            bwe[f] = descend(tiles, t_we)
            return c

        lax.fori_loop(0, F, one, 0)

    @pl.when(y_end & jnp.logical_not(x_end))
    def _():
        bwe[...] = jnp.zeros((F, KC, CY), f32)

    @pl.when(y_end)
    def _():
        def one(f, c):
            tiles = [psn[j // 2, f, 8 * (j % 2) : 8 * (j % 2) + 8] for j in range(16)]
            bsn[f] = descend(tiles, t_sn)
            return c

        lax.fori_loop(0, F, one, 0)

    @pl.when(x_end & jnp.logical_not(y_end))
    def _():
        bsn[...] = jnp.zeros((F, KC, CX), f32)

    @pl.when(x_end | y_end)
    def _():
        def one(f, c):
            b = bsn[f]
            for x in range(CX):
                for g in range(G):
                    v = xtab[x] * bwe[f, rows(g)] + wy * b[8 * g : 8 * g + 8, x : x + 1]
                    edge[f, x, rows(g)] = v
                    u1[f, x + 2, rows(g)] = u1[f, x + 2, rows(g)] + v
            return c

        lax.fori_loop(0, F, one, 0)

    await_y(R_U0)

    def settle_first(x, f, g):
        v = u1[f, x + 2, rows(g)] + dz[x, rows(g)] * mend(x, f, g)
        u1[f, x + 2, rows(g)] = v
        return v

    pack(R_U1, settle_first)
    ship_x(R_U1, u1)
    ship_y(R_U1)

    sweep(R_Q2, q2, functools.partial(retreat, mid, q2, out_g))

    sweep(R_U1, u1, functools.partial(advance, u1, out_f, 0))

    relay_gradients()

    @pl.when(x_end | y_end)
    def _():
        def one(f, c):
            for x in range(CX):
                out_f[f, x] = out_f[f, x] + edge[f, x]
            return c

        lax.fori_loop(0, F, one, 0)

    await_y(R_Q2)

    def settle_grad(x, g):
        for f in range(F):
            out_g[f, x, rows(g)] = out_g[f, x, rows(g)] + mend(x, f, g)

    per_group(range(CX), settle_grad)
    for x in range(CX):
        here(out_g.at[:, x], grad.at[:, :, x, :], L_GRAD).start()
    await_y(R_U1)

    def settle_final(x, g):
        for f in range(F):
            out_f[f, x, rows(g)] = out_f[f, x, rows(g)] + dz[x, rows(g)] * mend(x, f, g)

    per_group(range(CX), settle_final)
    for x in range(CX):
        here(out_f.at[:, x], final.at[:, :, x, :], L_FINAL).start()

    for r, ref in ((R_Q1, q1), (R_U0, u0), (R_Q2, q2), (R_U1, u1)):
        pair = ref.at[:, 0:2]
        for way, cond, what in (
            (LEFT, gx > 0, pair), (RIGHT, gx < nx - 1, pair),
            (DOWN, gy > 0, packs.at[r, 0]), (UP, gy < ny - 1, packs.at[r, 1]),
        ):
            @pl.when(cond)
            def _():
                whole(what, snd, 4 * r + way).wait()

    for e, sub in enumerate(subs):
        root = e * (nx - 1)

        @pl.when(gx != sub)
        def _():
            whole(pwe_in.at[e], snd, S_PWE + e).wait()
            whole(gwe.at[e], rcv, S_GWE + e).wait()

        @pl.when(gx == sub)
        def _():
            whole(gw.at[pl.ds(base + 1 - e, W - 1)], snd, S_GWE).wait()
            here(gw.at[gx], gwe.at[e], L_GWE).wait()

        @pl.when((gx == sub) & (gx != root))
        def _():
            whole(pwe.at[pl.ds(base, W)], snd, S_PWE2).wait()

        @pl.when(gx == root)
        def _():
            whole(gw.at[0 : nx - W] if e else gw.at[W:nx], snd, S_GWE2).wait()

        last = e * (ny - 1)

        @pl.when(gy != last)
        def _():
            whole(psn_in.at[e], snd, S_PSN + e).wait()
            whole(gsn.at[e], rcv, S_GSN + e).wait()

        @pl.when(gy == last)
        def _():
            whole(gs.at[0 : ny - 1] if e else gs.at[1:ny], snd, S_GSN).wait()
            here(gs.at[last], gsn.at[e], L_GSN).wait()

    whole(out_g, loc, L_GRAD).wait()
    whole(out_f, loc, L_FINAL).wait()


def store(*refs):
    sources, targets, stage, sems = refs[:4], refs[4:8], refs[8:12], refs[12]
    moves = []
    for i, (src, mid, dst) in enumerate(zip(sources, stage, targets, strict=True)):
        for f in range(F if i < 2 else 1):
            a, b, c = (src.at[f], mid.at[f], dst.at[f]) if i < 2 else (src, mid, dst)
            moves.append((pltpu.make_async_copy(a, b, sems.at[0, i, f]), pltpu.make_async_copy(b, c, sems.at[1, i, f])))
    for first, _ in moves:
        first.start()
    for first, second in moves:
        first.wait()
        second.start()
    for _, second in moves:
        second.wait()


def solution(mesh):
    nx, ny = mesh.shape["gx"], mesh.shape["gy"]
    wide, flat = (F, CX + 4, KC, CY), (F, CX, KC, CY)

    def body(*args):
        far = pl.BlockSpec(memory_space=pltpu.HBM)
        scratch = [wide] * 4 + [flat] * 5 + [
            (CX, KC, CY), (CX, KC, CY), (CX, 8, CY), (CX, 8, CY),
            (nx, F, KP // nx, CY), (ny, F, KP // ny, CX), (F, KC, CY), (F, KC, CX),
            (nx, F, KP // nx, CY), (ny, F, KP // ny, CX),
            (4, 2, 5, 8, CY), (4, 2, 5, 8, CY), (4, G, 3, 8, CY), (G, 3, 8, CY),
        ]
        native = jax.ShapeDtypeStruct((F, KC, CX, CY), f32)
        edges = (
            jax.ShapeDtypeStruct((2, F, KP // nx, CY), f32),
            jax.ShapeDtypeStruct((2, F, KP // ny, CX), f32),
        )
        results = pl.pallas_call(
            functools.partial(kernel, nx, ny),
            out_shape=(native, native, *edges),
            in_specs=[far] * 9,
            out_specs=[far] * 4,
            scratch_shapes=[pltpu.VMEM(s, f32) for s in scratch] + [
                pltpu.VMEM((2, CY), jnp.int32),
                pltpu.VMEM((2, CX), jnp.int32),
                pltpu.SMEM((F, F), f32),
                pltpu.VMEM((1, 1), jnp.int32),
                pltpu.SemaphoreType.DMA((13,)),
                pltpu.SemaphoreType.DMA((NSEM,)),
                pltpu.SemaphoreType.DMA((NSEM,)),
                pltpu.SemaphoreType.REGULAR,
                pltpu.SemaphoreType.REGULAR((2,)),
                pltpu.SemaphoreType.REGULAR((2,)),
            ],
            compiler_params=pltpu.CompilerParams(
                collective_id=0, has_side_effects=True, vmem_limit_bytes=VMEM_LIMIT
            ),
            name="nest",
        )(*args[:8], args[8].reshape(1, 1))
        return pl.pallas_call(
            store,
            out_shape=(native, native, *edges),
            in_specs=[far] * 4,
            out_specs=[far] * 4,
            scratch_shapes=[pltpu.VMEM(o.shape, f32) for o in (native, native, *edges)] + [pltpu.SemaphoreType.DMA((2, 4, F))],
            compiler_params=pltpu.CompilerParams(vmem_limit_bytes=VMEM_LIMIT),
            name="store",
        )(*results)

    return jax.shard_map(
        body,
        mesh=mesh,
        in_specs=(
            P(None, None, "gx", "gy"),
            P(None, None, "gx", "gy"),
            P(None, "gx", "gy"),
            P(),
            P(None, None, "gx", "gy"),
            P(None, None, "gy", "gx"),
            P(None, "gy"),
            P(None, "gx"),
            P(),
        ),
        out_specs=(
            P(None, None, "gx", "gy"),
            P(None, None, "gx", "gy"),
            P(None, None, "gx", "gy"),
            P(None, None, "gy", "gx"),
        ),
        check_vma=False,
    )
```

time: 47.2 us -> 41.3 us (0.87)
  the two profiles are of different devices: /device:TPU:6 before, /device:TPU:230 now
where the time goes in v2:
time: 41.3 us; the launch traced here: 41.2 us
  Pallas kernels  39.9 us (97%)
  between operations  1.29 us (3%)
    pallas_call x1, Pallas kernels, body(): pl.pallas_call(functools.partial(kernel, nx, ny), out_shape=(native, nati...  37.1 us
    pallas_call x1, Pallas kernels, body(): pl.pallas_call(store, out_shape=(native, native, *edges), in_specs=[far]...  2.81 us

profile of v2, /device:TPU:230, one launch (start us, length us, event | category | flops | bytes accessed | tf_op | source)
XLA Modules:
  0.0 41.2 jit_solution(17448521688960116112)
XLA Ops:
  1.3 37.1 %nest.1 = (f32[5,32,16,128]{3,2,1,0:T(8,128)}, f32[5,32,16,128]{3,2,1,0:T(8,128)}, f32[2,5,4,128]{3,2,1,0:T(4,128)}, f32[2,5,16,16]{3,2,1,0:T(8,128)}) custom-call(f32[5,32,16,128]{3,2,1,0:T(8,128)} %state.1, f32[5,32,16,128]{3,2,1,0:T(8,128)} %cot.1, f32[32,16,128]{2,1,0:T(8,128)} %dif.1, f32[5,5]{1,0:T(8,128)} %mix_in.1, f32[2,5,4,128]{3,2,1,0:T(4,128)} %pwe_in.1, ...), custom_call_target="tpu_custom_call" | custom-call | tf_op jit(solution)/shard_map/nest/pallas_call | solution.py:655
  38.3 2.8 %store.1 = (f32[5,32,16,128]{3,2,1,0:T(8,128)}, f32[5,32,16,128]{3,2,1,0:T(8,128)}, f32[2,5,4,128]{3,2,1,0:T(4,128)}, f32[2,5,16,16]{3,2,1,0:T(8,128)}) custom-call(f32[5,32,16,128]{3,2,1,0:T(8,128)} %get-tuple-element.8.refs_0_, f32[5,32,16,128]{3,2,1,0:T(8,128)} %get-tuple-element.9.refs_1_, f32[2,5,4,128]{3,2,1,0:T(4,128)} %get-tuple-element.10.refs_2_, ...), custom_call_target="tpu_custom_call" | custom-call | tf_op jit(solution)/shard_map/store/pallas_call | solution.py:677

commit v3 on v2

--- a/solution.py
+++ b/solution.py
@@ -10,15 +10,16 @@
 MESH = pl.DeviceIdType.MESH
 F, KC, KP, CX, CY = 5, 32, 128, 16, 128
 G = KC // 8
+INNER, OUTER = tuple(range(2, CX - 2)), (0, 1, CX - 2, CX - 1)
 f32 = jnp.float32
 
-L_COT, L_DIF, L_STATE, L_TWE, L_TSN, L_PWE, L_PSN, L_GWE, L_GSN, L_MIX, L_RW, L_GRAD, L_FINAL = range(13)
+L_COT, L_DIF, L_STATE, L_TWE, L_TSN, L_PWE, L_PSN, L_GWE, L_MIX, L_RW = range(10)
 R_Q1, R_U0, R_Q2, R_U1 = range(4)
 LEFT, RIGHT, DOWN, UP = range(4)
 S_PWE, S_PSN, S_GWE, S_GSN = 16, 18, 20, 22
 S_PWE2, S_GWE2 = 24, 25
 NSEM = 26
-VMEM_LIMIT = 56 * 2**20
+VMEM_LIMIT = 40 * 2**20
 W = 8
 
 
@@ -29,9 +30,9 @@
 def kernel(
     nx, ny,
     state, cot, dif, mix_in, pwe_in, psn_in, twe_in, tsn_in, rw_in,
-    final, grad, gwe, gsn,
-    u0, u1, q1, q2, a0, mid, out_f, out_g, edge, dp, dz, ztab, xtab,
-    pwe, psn, bwe, bsn, gw, gs, packs, heard, own, halo, twe, tsn, mix, rw,
+    out_f, out_g, gwe, gsn,
+    u0, u1, q1, q2, a0, mid, edge, dp, dz, ztab, xtab,
+    pwe, psv, psd, psn, bwe, bsn, gw, gs, gsd, packs, heard, own, halo, twe, tsn, mix, rw,
     loc, snd, rcv, above, opened, entered,
 ):
     gx, gy = lax.axis_index("gx"), lax.axis_index("gy")
@@ -72,6 +73,7 @@
     wanted = wanted + jnp.where(west & (gx > 0), 1, 0) + jnp.where(gx == nx - 1, nx // W - 1, 0)
 
     here(rw_in, rw, L_RW).start()
+    here(psn_in, psv, L_PSN).start()
     for x in range(CX):
         here(cot.at[:, :, x, :], a0.at[:, x], L_COT).start()
         here(dif.at[:, x, :], dp.at[x], L_DIF).start()
@@ -242,6 +244,32 @@
         for i in range(2):
             send(state.at[:, :, CX - 2 + i, :], u0.at[:, i], 4 * R_U0 + RIGHT, 4 * R_U0 + RIGHT, {"gx": gx + 1}).start()
 
+    piece = [(2 * f + h, f, h) for f in range(F) for h in range(2)]
+
+    def fill(block):
+        tiles = [jnp.zeros((8, CY), f32), jnp.zeros((8, CY), f32)]
+        for i, f, h in piece:
+            tiles[i // 8] = tiles[i // 8] + pltpu.roll(block(f, h), CX * (i % 8), 1)
+        return tiles
+
+    def unfill(ref, f, h):
+        i = 2 * f + h
+        return pltpu.roll(ref[i // 8], (CY - CX * (i % 8)) % CY, 1)
+
+    def widen(v):
+        wide = jnp.zeros((8, CY), v.dtype)
+        for x in range(CX):
+            wide = jnp.where(lane == x, v[:, x : x + 1], wide)
+        return wide
+
+    here(psn_in, psv, L_PSN).wait()
+    for e in range(2):
+        psd[e, 0], psd[e, 1] = fill(lambda f, h: widen(psv[e, f, 8 * h : 8 * h + 8]))
+
+        @pl.when(gy == e * (ny - 1))
+        def _():
+            psn[e * (ny - 1)] = psd[e]
+
     def signal(sem, axis, to):
         pl.semaphore_signal(sem, inc=1, device_id={axis: jnp.int32(to)}, device_id_type=MESH)
 
@@ -249,7 +277,7 @@
     def _():
         signal(above, "gy", gy - 1)
         signal(entered.at[1], "gy", 0)
-        send(psn_in.at[0], psn.at[gy], S_PSN, S_PSN, {"gy": jnp.int32(0)}).start()
+        send(psd.at[0], psn.at[gy], S_PSN, S_PSN, {"gy": jnp.int32(0)}).start()
 
     @pl.when(gy == ny - 1)
     def _():
@@ -291,10 +319,6 @@
         def _():
             here(pwe_in.at[e], pwe.at[gx], L_PWE).start()
 
-        @pl.when(gy == e * (ny - 1))
-        def _():
-            here(psn_in.at[e], psn.at[gy], L_PSN).start()
-
     whole(u0.at[:, 2 : CX + 2], loc, L_STATE).wait()
 
     pack(R_U0, lambda x, f, g: u0[f, x + 2, rows(g)])
@@ -324,11 +348,11 @@
             dst[f, x + shift, rows(g)] = z * (d * both[f][0] + blend(c, f, False))
 
     def sweep(r, ref, step, between=None):
-        per_group(range(2, CX - 2), step)
+        per_group(INNER, step)
         if between is not None:
             between()
         await_x(r, ref)
-        per_group((0, 1, CX - 2, CX - 1), step)
+        per_group(OUTER, step)
 
     def block_to(root):
         block = pwe.at[pl.ds(base, W)]
@@ -360,6 +384,14 @@
 
     ship_up(R_Q1, middle)
     ship_up(R_U0, middle)
+
+    def send_north(cond):
+        @pl.when(cond)
+        def _():
+            pl.semaphore_wait(opened.at[1], 1)
+            send(psd.at[1], psn.at[gy], S_PSN + 1, S_PSN + 1, {"gy": jnp.int32(ny - 1)}).start()
+
+    send_north((gy >= ny // 2 - 1) & (gy < ny - 1))
     await_y(R_Q1)
 
     def settle_middle(x, f, g):
@@ -397,7 +429,7 @@
         return arr[0:KC]
 
     t_we = jnp.broadcast_to(jnp.where(gx == 0, twe[0:1], twe[1:2]), (8, CY))
-    t_sn = jnp.broadcast_to(jnp.where(gy == 0, tsn[0:1], tsn[1:2]), (8, CX))
+    t_sn = widen(jnp.broadcast_to(jnp.where(gy == 0, tsn[0:1], tsn[1:2]), (8, CX)))
 
     @pl.when(x_end)
     def _():
@@ -418,21 +450,18 @@
 
     @pl.when(y_end)
     def _():
-        def one(f, c):
-            col = lax.broadcasted_iota(jnp.int32, (8, CX), 1)
+        sums = []
+        for f in range(F):
             d = []
             for g in range(G):
-                s = jnp.zeros((8, CX), f32)
+                t = jnp.zeros((8, CY), f32)
                 for x in range(CX):
                     v = jnp.sum(wy * (a0[f, x, rows(g)] + mid[f, x, rows(g)]), axis=1, keepdims=True)
-                    s = jnp.where(col == x, v, s)
-                d.append(s)
-            tiles = climb(jnp.concatenate(d, 0), t_sn, CX)
-            for j in range(16):
-                gs[j // 2, f, 8 * (j % 2) : 8 * (j % 2) + 8] = tiles[j]
-            return c
-
-        lax.fori_loop(0, F, one, 0)
+                    t = jnp.where(lane == x, v, t)
+                d.append(t)
+            sums.append(climb(jnp.concatenate(d, 0), t_sn, CY))
+        for j in range(ny):
+            gs[j, 0], gs[j, 1] = fill(lambda f, h: sums[f][2 * j + h])
 
     def spread_we(e):
         root = e * (nx - 1)
@@ -443,10 +472,10 @@
 
     def spread_sn(e):
         root = e * (ny - 1)
-        here(gs.at[root], gsn.at[e], L_GSN).start()
+        gsd[e] = gs[root]
         for j in range(ny):
             if j != root:
-                send(gs.at[j], gsn.at[e], S_GSN, S_GSN + e, {"gy": jnp.int32(j)}).start()
+                send(gs.at[j], gsd.at[e], S_GSN, S_GSN + e, {"gy": jnp.int32(j)}).start()
 
     for e in range(2):
         @pl.when(gx == e * (nx - 1))
@@ -473,10 +502,10 @@
                 for j in range(W - 1):
                     to = base + j + 1 - e
                     send(gw.at[to], gwe.at[e], S_GWE, S_GWE + e, {"gx": to}).start()
-    @pl.when(gy < ny - 1)
-    def _():
-        pl.semaphore_wait(opened.at[1], 1)
-        send(psn_in.at[1], psn.at[gy], S_PSN + 1, S_PSN + 1, {"gy": jnp.int32(ny - 1)}).start()
+    send_north((gy < ny // 2 - 1))
+
+    back = functools.partial(retreat, mid, q2, out_g)
+    per_group(INNER, back)
 
     for e in range(2):
         @pl.when(gx == e * (nx - 1))
@@ -486,7 +515,6 @@
         @pl.when(gy == e * (ny - 1))
         def _():
             whole(psn.at[0 : ny - 1] if e else psn.at[1:ny], rcv, S_PSN + e).wait()
-            here(psn_in.at[e], psn.at[gy], L_PSN).wait()
 
     @pl.when(x_end)
     def _():
@@ -503,16 +531,12 @@
 
     @pl.when(y_end)
     def _():
-        def one(f, c):
-            tiles = [psn[j // 2, f, 8 * (j % 2) : 8 * (j % 2) + 8] for j in range(16)]
-            bsn[f] = descend(tiles, t_sn)
-            return c
-
-        lax.fori_loop(0, F, one, 0)
+        for f in range(F):
+            bsn[f] = descend([unfill(psn.at[j // 2], f, j % 2) for j in range(16)], t_sn)
 
     @pl.when(x_end & jnp.logical_not(y_end))
     def _():
-        bsn[...] = jnp.zeros((F, KC, CX), f32)
+        bsn[...] = jnp.zeros((F, KC, CY), f32)
 
     @pl.when(x_end | y_end)
     def _():
@@ -538,11 +562,12 @@
     ship_x(R_U1, u1)
     ship_y(R_U1)
 
-    sweep(R_Q2, q2, functools.partial(retreat, mid, q2, out_g))
+    await_x(R_Q2, q2)
+    per_group(OUTER, back)
+
+    relay_gradients()
 
     sweep(R_U1, u1, functools.partial(advance, u1, out_f, 0))
-
-    relay_gradients()
 
     @pl.when(x_end | y_end)
     def _():
@@ -560,8 +585,6 @@
             out_g[f, x, rows(g)] = out_g[f, x, rows(g)] + mend(x, f, g)
 
     per_group(range(CX), settle_grad)
-    for x in range(CX):
-        here(out_g.at[:, x], grad.at[:, :, x, :], L_GRAD).start()
     await_y(R_U1)
 
     def settle_final(x, g):
@@ -569,8 +592,6 @@
             out_f[f, x, rows(g)] = out_f[f, x, rows(g)] + dz[x, rows(g)] * mend(x, f, g)
 
     per_group(range(CX), settle_final)
-    for x in range(CX):
-        here(out_f.at[:, x], final.at[:, :, x, :], L_FINAL).start()
 
     for r, ref in ((R_Q1, q1), (R_U0, u0), (R_Q2, q2), (R_U1, u1)):
         pair = ref.at[:, 0:2]
@@ -607,32 +628,27 @@
 
         @pl.when(gy != last)
         def _():
-            whole(psn_in.at[e], snd, S_PSN + e).wait()
-            whole(gsn.at[e], rcv, S_GSN + e).wait()
+            whole(psd.at[e], snd, S_PSN + e).wait()
+            whole(gsd.at[e], rcv, S_GSN + e).wait()
 
         @pl.when(gy == last)
         def _():
             whole(gs.at[0 : ny - 1] if e else gs.at[1:ny], snd, S_GSN).wait()
-            here(gs.at[last], gsn.at[e], L_GSN).wait()
-
-    whole(out_g, loc, L_GRAD).wait()
-    whole(out_f, loc, L_FINAL).wait()
-
-
-def store(*refs):
-    sources, targets, stage, sems = refs[:4], refs[4:8], refs[8:12], refs[12]
-    moves = []
-    for i, (src, mid, dst) in enumerate(zip(sources, stage, targets, strict=True)):
-        for f in range(F if i < 2 else 1):
-            a, b, c = (src.at[f], mid.at[f], dst.at[f]) if i < 2 else (src, mid, dst)
-            moves.append((pltpu.make_async_copy(a, b, sems.at[0, i, f]), pltpu.make_async_copy(b, c, sems.at[1, i, f])))
-    for first, _ in moves:
-        first.start()
-    for first, second in moves:
-        first.wait()
-        second.start()
-    for _, second in moves:
-        second.wait()
+
+        for _, f, h in piece:
+            gsn[e, f, 8 * h : 8 * h + 8] = unfill(gsd.at[e], f, h)[:, 0:CX]
+
+
+def store(out_f, out_g, gwe, gsn, final, grad, gwe_out, gsn_out, sems):
+    copies = [pltpu.make_async_copy(gwe, gwe_out, sems.at[2]), pltpu.make_async_copy(gsn, gsn_out, sems.at[3])]
+    for c in copies:
+        c.start()
+    for i, (src, dst) in enumerate(((out_f, final), (out_g, grad))):
+        for x in range(CX):
+            pltpu.make_async_copy(src.at[:, x], dst.at[:, :, x, :], sems.at[i]).start()
+        copies.append(pltpu.make_async_copy(src, src, sems.at[i]))
+    for c in copies:
+        c.wait()
 
 
 def solution(mesh):
@@ -640,13 +656,14 @@
     wide, flat = (F, CX + 4, KC, CY), (F, CX, KC, CY)
 
     def body(*args):
-        far = pl.BlockSpec(memory_space=pltpu.HBM)
-        scratch = [wide] * 4 + [flat] * 5 + [
+        far, near = pl.BlockSpec(memory_space=pltpu.HBM), pl.BlockSpec(memory_space=pltpu.VMEM)
+        scratch = [wide] * 4 + [flat] * 3 + [
             (CX, KC, CY), (CX, KC, CY), (CX, 8, CY), (CX, 8, CY),
-            (nx, F, KP // nx, CY), (ny, F, KP // ny, CX), (F, KC, CY), (F, KC, CX),
-            (nx, F, KP // nx, CY), (ny, F, KP // ny, CX),
+            (nx, F, KP // nx, CY), (2, F, KP // ny, CX), (2, 2, 8, CY), (ny, 2, 8, CY), (F, KC, CY), (F, KC, CY),
+            (nx, F, KP // nx, CY), (ny, 2, 8, CY), (2, 2, 8, CY),
             (4, 2, 5, 8, CY), (4, 2, 5, 8, CY), (4, G, 3, 8, CY), (G, 3, 8, CY),
         ]
+        child = jax.ShapeDtypeStruct(flat, f32)
         native = jax.ShapeDtypeStruct((F, KC, CX, CY), f32)
         edges = (
             jax.ShapeDtypeStruct((2, F, KP // nx, CY), f32),
@@ -654,15 +671,15 @@
         )
         results = pl.pallas_call(
             functools.partial(kernel, nx, ny),
-            out_shape=(native, native, *edges),
+            out_shape=(child, child, *edges),
             in_specs=[far] * 9,
-            out_specs=[far] * 4,
+            out_specs=[near] * 4,
             scratch_shapes=[pltpu.VMEM(s, f32) for s in scratch] + [
                 pltpu.VMEM((2, CY), jnp.int32),
                 pltpu.VMEM((2, CX), jnp.int32),
                 pltpu.SMEM((F, F), f32),
                 pltpu.VMEM((1, 1), jnp.int32),
-                pltpu.SemaphoreType.DMA((13,)),
+                pltpu.SemaphoreType.DMA((10,)),
                 pltpu.SemaphoreType.DMA((NSEM,)),
                 pltpu.SemaphoreType.DMA((NSEM,)),
                 pltpu.SemaphoreType.REGULAR,
@@ -673,13 +690,13 @@
                 collective_id=0, has_side_effects=True, vmem_limit_bytes=VMEM_LIMIT
             ),
             name="nest",
-        )(*args[:8], args[8].reshape(1, 1))
+        )(*[pltpu.with_memory_space_constraint(a, pltpu.HBM) for a in args[:8]], args[8].reshape(1, 1))
         return pl.pallas_call(
             store,
             out_shape=(native, native, *edges),
-            in_specs=[far] * 4,
+            in_specs=[near] * 4,
             out_specs=[far] * 4,
-            scratch_shapes=[pltpu.VMEM(o.shape, f32) for o in (native, native, *edges)] + [pltpu.SemaphoreType.DMA((2, 4, F))],
+            scratch_shapes=[pltpu.SemaphoreType.DMA((4,))],
             compiler_params=pltpu.CompilerParams(vmem_limit_bytes=VMEM_LIMIT),
             name="store",
         )(*results)

time: 41.3 us -> 34.6 us (0.84)
  the two profiles are of different devices: /device:TPU:230 before, /device:TPU:95 now
where the time goes in v3:
time: 34.6 us; the launch traced here: 34.5 us
  Pallas kernels  33.2 us (96%)
  between operations  1.29 us (4%)
    pallas_call x1, Pallas kernels, body(): pl.pallas_call(functools.partial(kernel, nx, ny), out_shape=(child, child...  31.6 us
    pallas_call x1, Pallas kernels, body(): pl.pallas_call(store, out_shape=(native, native, *edges), in_specs=[near]...  1.54 us

profile of v3, /device:TPU:95, one launch (start us, length us, event | category | flops | bytes accessed | tf_op | source)
XLA Modules:
  0.0 34.5 jit_solution(8919634439336453396)
XLA Ops:
  1.3 31.6 %nest.1 = (f32[5,16,32,128]{3,2,1,0:T(8,128)S(1)}, f32[5,16,32,128]{3,2,1,0:T(8,128)S(1)}, f32[2,5,4,128]{3,2,1,0:T(4,128)S(1)}, f32[2,5,16,16]{3,2,1,0:T(8,128)S(1)}) custom-call(f32[5,32,16,128]{3,2,1,0:T(8,128)} %state.1, f32[5,32,16,128]{3,2,1,0:T(8,128)} %cot.1, f32[32,16,128]{2,1,0:T(8,128)} %dif.1, f32[5,5]{1,0:T(8,128)} %mix_in.1, ...), custom_call_target="tpu_custom_call" | custom-call | tf_op jit(solution)/shard_map/nest/pallas_call | solution.py:672
  32.9 1.5 %store.1 = (f32[5,32,16,128]{3,2,1,0:T(8,128)}, f32[5,32,16,128]{3,2,1,0:T(8,128)}, f32[2,5,4,128]{3,2,1,0:T(4,128)}, f32[2,5,16,16]{3,2,1,0:T(8,128)}) custom-call(f32[5,16,32,128]{3,2,1,0:T(8,128)S(1)} %get-tuple-element.8.out_f, f32[5,16,32,128]{3,2,1,0:T(8,128)S(1)} %get-tuple-element.9.out_g, f32[2,5,4,128]{3,2,1,0:T(4,128)S(1)} %get-tuple-element.10.gwe, ...), custom_call_target="tpu_custom_call" | custom-call | tf_op jit(solution)/shard_map/store/pallas_call | solution.py:694

commit v4 on v3

--- a/solution.py
+++ b/solution.py
@@ -234,6 +234,29 @@
         lax.fori_loop(0, G, one, 0)
 
     pl.semaphore_wait(barrier, wanted)
+
+    def signal(sem, axis, to):
+        pl.semaphore_signal(sem, inc=1, device_id={axis: jnp.int32(to)}, device_id_type=MESH)
+
+    @pl.when(gy > 0)
+    def _():
+        signal(above, "gy", gy - 1)
+        signal(entered.at[1], "gy", 0)
+
+    @pl.when(gy == ny - 1)
+    def _():
+        for i in range(ny - 1):
+            signal(opened.at[1], "gy", i)
+
+    @pl.when(west & (gx > 0))
+    def _():
+        signal(entered.at[0], "gx", 0)
+
+    @pl.when(gx == nx - 1)
+    def _():
+        for i in range(W - 1, nx - 1, W):
+            signal(opened.at[0], "gx", i)
+
     @pl.when(gx > 0)
     def _():
         for i in range(2):
@@ -243,55 +266,6 @@
     def _():
         for i in range(2):
             send(state.at[:, :, CX - 2 + i, :], u0.at[:, i], 4 * R_U0 + RIGHT, 4 * R_U0 + RIGHT, {"gx": gx + 1}).start()
-
-    piece = [(2 * f + h, f, h) for f in range(F) for h in range(2)]
-
-    def fill(block):
-        tiles = [jnp.zeros((8, CY), f32), jnp.zeros((8, CY), f32)]
-        for i, f, h in piece:
-            tiles[i // 8] = tiles[i // 8] + pltpu.roll(block(f, h), CX * (i % 8), 1)
-        return tiles
-
-    def unfill(ref, f, h):
-        i = 2 * f + h
-        return pltpu.roll(ref[i // 8], (CY - CX * (i % 8)) % CY, 1)
-
-    def widen(v):
-        wide = jnp.zeros((8, CY), v.dtype)
-        for x in range(CX):
-            wide = jnp.where(lane == x, v[:, x : x + 1], wide)
-        return wide
-
-    here(psn_in, psv, L_PSN).wait()
-    for e in range(2):
-        psd[e, 0], psd[e, 1] = fill(lambda f, h: widen(psv[e, f, 8 * h : 8 * h + 8]))
-
-        @pl.when(gy == e * (ny - 1))
-        def _():
-            psn[e * (ny - 1)] = psd[e]
-
-    def signal(sem, axis, to):
-        pl.semaphore_signal(sem, inc=1, device_id={axis: jnp.int32(to)}, device_id_type=MESH)
-
-    @pl.when(gy > 0)
-    def _():
-        signal(above, "gy", gy - 1)
-        signal(entered.at[1], "gy", 0)
-        send(psd.at[0], psn.at[gy], S_PSN, S_PSN, {"gy": jnp.int32(0)}).start()
-
-    @pl.when(gy == ny - 1)
-    def _():
-        for i in range(ny - 1):
-            signal(opened.at[1], "gy", i)
-
-    @pl.when(west & (gx > 0))
-    def _():
-        signal(entered.at[0], "gx", 0)
-
-    @pl.when(gx == nx - 1)
-    def _():
-        for i in range(W - 1, nx - 1, W):
-            signal(opened.at[0], "gx", i)
 
     whole(dp, loc, L_DIF).wait()
     whole(a0, loc, L_COT).wait()
@@ -308,8 +282,8 @@
     per_group(range(CX), first)
     pack(R_Q1, lambda x, f, g: q1[f, x + 2, rows(g)])
 
+    ship_y(R_Q1)
     ship_x(R_Q1, q1)
-    ship_y(R_Q1)
     for e, sub in enumerate(subs):
         @pl.when(gx != sub)
         def _():
@@ -318,6 +292,33 @@
         @pl.when(gx == sub)
         def _():
             here(pwe_in.at[e], pwe.at[gx], L_PWE).start()
+
+    piece = [(2 * f + h, f, h) for f in range(F) for h in range(2)]
+
+    def fill(block):
+        tiles = [jnp.zeros((8, CY), f32), jnp.zeros((8, CY), f32)]
+        for i, f, h in piece:
+            tiles[i // 8] = tiles[i // 8] + pltpu.roll(block(f, h), CX * (i % 8), 1)
+        return tiles
+
+    def unfill(ref, f, h):
+        i = 2 * f + h
+        return pltpu.roll(ref[i // 8], (CY - CX * (i % 8)) % CY, 1)
+
+    def widen(v):
+        return jnp.concatenate([v, jnp.zeros((8, CY - CX), v.dtype)], 1)
+
+    here(psn_in, psv, L_PSN).wait()
+    for e in range(2):
+        psd[e, 0], psd[e, 1] = fill(lambda f, h: widen(psv[e, f, 8 * h : 8 * h + 8]))
+
+        @pl.when(gy == e * (ny - 1))
+        def _():
+            psn[e * (ny - 1)] = psd[e]
+
+    @pl.when(gy > 0)
+    def _():
+        send(psd.at[0], psn.at[gy], S_PSN, S_PSN, {"gy": jnp.int32(0)}).start()
 
     whole(u0.at[:, 2 : CX + 2], loc, L_STATE).wait()
 
@@ -376,22 +377,16 @@
 
     sweep(R_U0, u0, functools.partial(advance, u0, u1, 2))
 
-    middle = gy == ny // 2 - 1
-    ship_up(R_Q1, (gy < ny - 1) & jnp.logical_not(middle))
-    ship_up(R_U0, (gy < ny - 1) & jnp.logical_not(middle))
+    ship_up(R_Q1, gy < ny - 1)
+    ship_up(R_U0, gy < ny - 1)
 
     sweep(R_Q1, q1, functools.partial(retreat, a0, q1, mid), take_columns)
 
-    ship_up(R_Q1, middle)
-    ship_up(R_U0, middle)
-
-    def send_north(cond):
-        @pl.when(cond)
-        def _():
-            pl.semaphore_wait(opened.at[1], 1)
-            send(psd.at[1], psn.at[gy], S_PSN + 1, S_PSN + 1, {"gy": jnp.int32(ny - 1)}).start()
-
-    send_north((gy >= ny // 2 - 1) & (gy < ny - 1))
+    @pl.when(gy < ny - 1)
+    def _():
+        pl.semaphore_wait(opened.at[1], 1)
+        send(psd.at[1], psn.at[gy], S_PSN + 1, S_PSN + 1, {"gy": jnp.int32(ny - 1)}).start()
+
     await_y(R_Q1)
 
     def settle_middle(x, f, g):
@@ -402,8 +397,8 @@
         return v
 
     pack(R_Q2, settle_middle)
+    ship_y(R_Q2)
     ship_x(R_Q2, q2)
-    ship_y(R_Q2)
     here(twe_in, twe, L_TWE).wait()
     here(tsn_in, tsn, L_TSN).wait()
 
@@ -502,8 +497,6 @@
                 for j in range(W - 1):
                     to = base + j + 1 - e
                     send(gw.at[to], gwe.at[e], S_GWE, S_GWE + e, {"gx": to}).start()
-    send_north((gy < ny // 2 - 1))
-
     back = functools.partial(retreat, mid, q2, out_g)
     per_group(INNER, back)
 
@@ -559,8 +552,8 @@
         return v
 
     pack(R_U1, settle_first)
+    ship_y(R_U1)
     ship_x(R_U1, u1)
-    ship_y(R_U1)
 
     await_x(R_Q2, q2)
     per_group(OUTER, back)

time: 34.6 us -> 32.5 us (0.939)
  the two profiles are of different devices: /device:TPU:95 before, /device:TPU:6 now
where the time goes in v4:
time: 32.5 us; the launch traced here: 32.3 us
  Pallas kernels  31 us (95%)
  between operations  1.29 us (4%)
    pallas_call x1, Pallas kernels, body(): pl.pallas_call(functools.partial(kernel, nx, ny), out_shape=(child, child...  29.5 us
    pallas_call x1, Pallas kernels, body(): pl.pallas_call(store, out_shape=(native, native, *edges), in_specs=[near]...  1.54 us

profile of v4, /device:TPU:6, one launch (start us, length us, event | category | flops | bytes accessed | tf_op | source)
XLA Modules:
  0.0 32.3 jit_solution(5198497583397503439)
XLA Ops:
  1.3 29.5 %nest.1 = (f32[5,16,32,128]{3,2,1,0:T(8,128)S(1)}, f32[5,16,32,128]{3,2,1,0:T(8,128)S(1)}, f32[2,5,4,128]{3,2,1,0:T(4,128)S(1)}, f32[2,5,16,16]{3,2,1,0:T(8,128)S(1)}) custom-call(f32[5,32,16,128]{3,2,1,0:T(8,128)} %state.1, f32[5,32,16,128]{3,2,1,0:T(8,128)} %cot.1, f32[32,16,128]{2,1,0:T(8,128)} %dif.1, f32[5,5]{1,0:T(8,128)} %mix_in.1, ...), custom_call_target="tpu_custom_call" | custom-call | tf_op jit(solution)/shard_map/nest/pallas_call | solution.py:665
  30.8 1.5 %store.1 = (f32[5,32,16,128]{3,2,1,0:T(8,128)}, f32[5,32,16,128]{3,2,1,0:T(8,128)}, f32[2,5,4,128]{3,2,1,0:T(4,128)}, f32[2,5,16,16]{3,2,1,0:T(8,128)}) custom-call(f32[5,16,32,128]{3,2,1,0:T(8,128)S(1)} %get-tuple-element.8.out_f, f32[5,16,32,128]{3,2,1,0:T(8,128)S(1)} %get-tuple-element.9.out_g, f32[2,5,4,128]{3,2,1,0:T(4,128)S(1)} %get-tuple-element.10.gwe, ...), custom_call_target="tpu_custom_call" | custom-call | tf_op jit(solution)/shard_map/store/pallas_call | solution.py:687

commit v5 on v4

--- a/solution.py
+++ b/solution.py
@@ -498,7 +498,10 @@
                     to = base + j + 1 - e
                     send(gw.at[to], gwe.at[e], S_GWE, S_GWE + e, {"gx": to}).start()
     back = functools.partial(retreat, mid, q2, out_g)
-    per_group(INNER, back)
+
+    @pl.when(y_end)
+    def _():
+        per_group(INNER, back)
 
     for e in range(2):
         @pl.when(gx == e * (nx - 1))
@@ -554,6 +557,10 @@
     pack(R_U1, settle_first)
     ship_y(R_U1)
     ship_x(R_U1, u1)
+
+    @pl.when(jnp.logical_not(y_end))
+    def _():
+        per_group(INNER, back)
 
     await_x(R_Q2, q2)
     per_group(OUTER, back)

time: 32.5 us -> 32.1 us (0.988)
    pallas_call x1, Pallas kernels: 29.5 us -> 29.1 us  [body(): pl.pallas_call(functools.partial(kernel, nx, ny), out_shape=(child, child...]
where the time goes in v5:
time: 32.1 us; the launch traced here: 32 us
  Pallas kernels  30.7 us (96%)
  between operations  1.29 us (4%)
    pallas_call x1, Pallas kernels, body(): pl.pallas_call(functools.partial(kernel, nx, ny), out_shape=(child, child...  29.1 us
    pallas_call x1, Pallas kernels, body(): pl.pallas_call(store, out_shape=(native, native, *edges), in_specs=[near]...  1.54 us

profile of v5, /device:TPU:6, one launch (start us, length us, event | category | flops | bytes accessed | tf_op | source)
XLA Modules:
  0.0 32.0 jit_solution(17048421702314593907)
XLA Ops:
  1.3 29.1 %nest.1 = (f32[5,16,32,128]{3,2,1,0:T(8,128)S(1)}, f32[5,16,32,128]{3,2,1,0:T(8,128)S(1)}, f32[2,5,4,128]{3,2,1,0:T(4,128)S(1)}, f32[2,5,16,16]{3,2,1,0:T(8,128)S(1)}) custom-call(f32[5,32,16,128]{3,2,1,0:T(8,128)} %state.1, f32[5,32,16,128]{3,2,1,0:T(8,128)} %cot.1, f32[32,16,128]{2,1,0:T(8,128)} %dif.1, f32[5,5]{1,0:T(8,128)} %mix_in.1, ...), custom_call_target="tpu_custom_call" | custom-call | tf_op jit(solution)/shard_map/nest/pallas_call | solution.py:672
  30.4 1.5 %store.1 = (f32[5,32,16,128]{3,2,1,0:T(8,128)}, f32[5,32,16,128]{3,2,1,0:T(8,128)}, f32[2,5,4,128]{3,2,1,0:T(4,128)}, f32[2,5,16,16]{3,2,1,0:T(8,128)}) custom-call(f32[5,16,32,128]{3,2,1,0:T(8,128)S(1)} %get-tuple-element.8.out_f, f32[5,16,32,128]{3,2,1,0:T(8,128)S(1)} %get-tuple-element.9.out_g, f32[2,5,4,128]{3,2,1,0:T(4,128)S(1)} %get-tuple-element.10.gwe, ...), custom_call_target="tpu_custom_call" | custom-call | tf_op jit(solution)/shard_map/store/pallas_call | solution.py:694
